TPU v7x, 256 devices: a whole 4x4x8 slice. The times are simulated.
256 devices in a mesh: ctx: 32 (over x, z), hx: 8 (over y, core).
Axes of the slice: x: 4, y: 4, z: 8, core: 2. Of those that a mesh axis runs over, the one named last changes fastest.
Arguments:
- query_latent: bfloat16 [16, 128, 512], P(None, 'hx'), may hold values from -2 to 2
- query_rope: bfloat16 [16, 8192], P(None, 'hx'), may hold values from -80 to 80
- cache_latent: bfloat16 [4, 131072, 512], P(None, ('ctx', 'hx')), may hold values from -16 to 16
- cache_rope: bfloat16 [4, 64, 131072], P(None, None, ('ctx', 'hx')), may hold values from -8 to 8
- suffix_latent: bfloat16 [16, 32768, 512], P(None, ('ctx', 'hx')), may hold values from -16 to 16
- suffix_rope: bfloat16 [16, 64, 32768], P(None, None, ('ctx', 'hx')), may hold values from -6 to 6
- lengths: int32 [4], replicated, may hold values from 32768 to 131072, as said below
- parents: int32 [16], replicated, may hold values from 0 to 15, as said below
- w_uv: bfloat16 [512, 16384], P(None, ('ctx', 'hx')), may hold values from -1.25 to 1.25
- w_o: bfloat16 [16384, 7168], P(('ctx', 'hx')), may hold values from -0.046875 to 0.046875
- hidden: bfloat16 [16, 7168], replicated, may hold values from -6 to 6
- norm_gain: float32 [7168], replicated, may hold values from 0.1 to 1.9
- w_gate: bfloat16 [32768, 7168], P(('ctx', 'hx')), may hold values from -0.0625 to 0.0625
- w_up: bfloat16 [32768, 7168], P(('ctx', 'hx')), may hold values from -0.0625 to 0.0625
- w_down: bfloat16 [32768, 7168], P(('ctx', 'hx')), may hold values from -0.5 to 0.5
- expert_ids: int32 [16, 8], replicated, may hold values from 0 to 15, all different within a row
- gate_weights: float32 [16, 8], replicated, may hold values from 0.1 to 0.6
Outputs:
- attended: bfloat16 [16, 7168], replicated
- updated: bfloat16 [16, 7168], P(None, ('ctx', 'hx'))
Inputs may be any that keep to these rules, and one draw needn't show every extreme that they name: `lengths`: one request has length 131072 and another 131072 // 4. parents[b] is a hypothesis of the same request as b. `expert_ids`: each row names 8 different experts.
All inputs are finite; a program needn't handle non-finite values.
Results may differ from a plain program's by a relative error of at most 0.012.
Values may be sent and summed in bfloat16 or wider, within the bound.
A program may use at most 64 MiB of HBM per device.

v0:
```python
from functools import partial
import math

import jax
import jax.numpy as jnp
from jax import lax
from jax.sharding import PartitionSpec as P

DL = 512
DR = 64
DN = 128
DV = 128
EFF = 2048
REQ = 4
BEAMS = 4
HYPS = 16


MSCALE = 1.0 + 0.1 * math.log(40.0)
NEG = -1e30


def merged(value, axis, join):
    pieces = jax.tree.map(lambda part: lax.all_gather(part, axis), value)
    head = jax.tree.map(lambda part: part[0], pieces)
    tail = jax.tree.map(lambda part: part[1:], pieces)
    subtotal, _ = lax.scan(lambda subtotal, section: (join(subtotal, section), None), head, tail)
    return subtotal


def merge_pair(first_set, second_set):
    max_a, sum_a, acc_a = first_set
    max_b, sum_b, acc_b = second_set
    new_max = jnp.maximum(max_a, max_b)
    factor_a = jnp.exp(max_a - new_max)
    factor_b = jnp.exp(max_b - new_max)
    return (
        new_max,
        sum_a * factor_a + sum_b * factor_b,
        acc_a * factor_a[..., None] + acc_b * factor_b[..., None],
    )


def request_stats(
    q_lat, q_rope, pre_lat, pre_rope, suf_lat, suf_rope, is_live, softmax_scale, with_prefix
):
    suf_scores = jnp.einsum("bhl,bsl->bhs", q_lat, suf_lat, preferred_element_type=jnp.float32)
    suf_scores = (
        suf_scores
        + jnp.einsum("bhr,brs->bhs", q_rope, suf_rope, preferred_element_type=jnp.float32)
    ) * softmax_scale
    row_max = jnp.max(suf_scores, axis=2)
    beam_count, head_count, lat_width = q_lat.shape
    flat_lat = q_lat.reshape(beam_count * head_count, lat_width)
    flat_rope = q_rope.reshape(beam_count * head_count, q_rope.shape[2])
    pre_scores = lax.dot_general(
        flat_lat, pre_lat, (((1,), (1,)), ((), ())), preferred_element_type=jnp.float32
    )
    pre_scores = pre_scores + jnp.dot(flat_rope, pre_rope, preferred_element_type=jnp.float32)
    pre_scores = jnp.where(is_live[None, :], pre_scores * softmax_scale, NEG).reshape(
        beam_count, head_count, -1
    )
    row_max = jnp.maximum(row_max, jnp.max(pre_scores, axis=2))
    suf_weights = jnp.exp(suf_scores - row_max[..., None]).astype(jnp.bfloat16)
    weight_sum = jnp.sum(suf_weights.astype(jnp.float32), axis=2)
    weighted = jnp.einsum("bhs,bsl->bhl", suf_weights, suf_lat, preferred_element_type=jnp.float32)
    pre_weights = jnp.exp(pre_scores - row_max[..., None]).astype(jnp.bfloat16)
    weight_sum = weight_sum + jnp.sum(pre_weights.astype(jnp.float32), axis=2)
    prefix_part = jnp.dot(
        pre_weights.reshape(beam_count * head_count, -1),
        pre_lat,
        preferred_element_type=jnp.float32,
    )
    weighted = weighted + prefix_part.reshape(beam_count, head_count, lat_width)
    return (row_max, weight_sum, weighted)


def local(
    query_latent,
    query_rope,
    cache_latent,
    cache_rope,
    suffix_latent,
    suffix_rope,
    lengths,
    parents,
    w_uv,
    w_o,
    hidden,
    norm_gain,
    w_gate,
    w_up,
    w_down,
    expert_ids,
    gate_weights,
):
    q_lat, q_rope = (
        lax.all_gather(query_latent, "hx", axis=1, tiled=True),
        lax.all_gather(query_rope, "hx", axis=1, tiled=True),
    )
    head_count = q_lat.shape[1]
    q_rope = q_rope.reshape(HYPS, head_count, DR)
    softmax_scale = MSCALE * MSCALE / math.sqrt(DN + DR)
    n_hx = lax.axis_size("hx")
    linear = lax.axis_index("ctx") * n_hx + lax.axis_index("hx")
    ctx_block = cache_latent.shape[1]
    offsets = linear * ctx_block + jnp.arange(ctx_block, dtype=jnp.int32)
    suf_lat = jnp.take(suffix_latent, parents, axis=0)
    suf_rope = jnp.take(suffix_rope, parents, axis=0)
    maxima = []
    totals_list = []
    sums_list = []
    for request in range(REQ):
        hyp_rows = slice(request * BEAMS, (request + 1) * BEAMS)
        is_live = offsets < lengths[request]
        bound_stats = partial(
            request_stats,
            q_lat[hyp_rows],
            q_rope[hyp_rows],
            cache_latent[request],
            cache_rope[request],
            suf_lat[hyp_rows],
            suf_rope[hyp_rows],
            is_live,
            softmax_scale,
        )
        request_sums = bound_stats(True)
        maxima.append(request_sums[0])
        totals_list.append(request_sums[1])
        sums_list.append(request_sums[2])
    row_max = jnp.concatenate(maxima, axis=0)
    weight_sum = jnp.concatenate(totals_list, axis=0)
    weighted = jnp.concatenate(sums_list, axis=0)
    part_max, part_sum, part_acc = (
        lax.all_to_all(row_max[None], "ctx", split_axis=2, concat_axis=0, tiled=True),
        lax.all_to_all(weight_sum[None], "ctx", split_axis=2, concat_axis=0, tiled=True),
        lax.all_to_all(weighted[None], "ctx", split_axis=2, concat_axis=0, tiled=True),
    )
    group_max = jnp.max(part_max, axis=0)
    factor = jnp.exp(part_max - group_max[None])
    group_sum = jnp.sum(part_sum * factor, axis=0)
    group_acc = jnp.sum(part_acc * factor[..., None], axis=0)
    group_max, group_sum, group_acc = merged((group_max, group_sum, group_acc), "hx", merge_pair)
    attention = (group_acc / group_sum[..., None]).astype(jnp.bfloat16)
    columns = w_uv.shape[1]
    head_span = max(1, columns // DV)
    first_head = lax.axis_index("hx") * columns // DV
    chosen = lax.dynamic_slice_in_dim(attention, first_head, head_span, 1)
    value_map = w_uv.reshape(DL, head_span, columns // head_span)
    values = jnp.einsum("bnl,lnc->bnc", chosen, value_map, preferred_element_type=jnp.float32)
    values = values.astype(jnp.bfloat16).reshape(HYPS, columns)
    partial_out = jnp.dot(values, w_o, preferred_element_type=jnp.float32)
    attended = lax.psum(partial_out, ("ctx", "hx")).astype(jnp.bfloat16)
    residual = hidden.astype(jnp.float32) + attended.astype(jnp.float32)
    mean_square = jnp.mean(residual * residual, axis=1, keepdims=True)
    normed = (residual * lax.rsqrt(mean_square + 1e-06) * norm_gain).astype(jnp.bfloat16)
    unit_count = w_gate.shape[0]
    expert_here = linear * unit_count // EFF
    routed = jnp.sum(gate_weights * (expert_ids == expert_here).astype(jnp.float32), axis=1)
    gate_out = lax.dot_general(
        normed, w_gate, (((1,), (1,)), ((), ())), preferred_element_type=jnp.float32
    )
    up_out = lax.dot_general(
        normed, w_up, (((1,), (1,)), ((), ())), preferred_element_type=jnp.float32
    )
    activated = (jax.nn.silu(gate_out) * up_out * routed[:, None]).astype(jnp.bfloat16)
    expert_terms = jnp.dot(activated, w_down, preferred_element_type=jnp.float32)
    moe_share = lax.psum_scatter(expert_terms, ("ctx", "hx"), scatter_dimension=1, tiled=True)
    share_width = moe_share.shape[1]
    residual_share = lax.dynamic_slice_in_dim(residual, linear * share_width, share_width, 1)
    updated = (residual_share + moe_share).astype(jnp.bfloat16)
    return (attended, updated)


def solution(mesh):
    in_specs = (
        P(None, "hx", None),
        P(None, "hx"),
        P(None, ("ctx", "hx"), None),
        P(None, None, ("ctx", "hx")),
        P(None, ("ctx", "hx"), None),
        P(None, None, ("ctx", "hx")),
        P(),
        P(),
        P(None, ("ctx", "hx")),
        P(("ctx", "hx"), None),
        P(),
        P(),
        P(("ctx", "hx"), None),
        P(("ctx", "hx"), None),
        P(("ctx", "hx"), None),
        P(),
        P(),
    )
    out_specs = (P(), P(None, ("ctx", "hx")))
    return jax.shard_map(local, mesh=mesh, in_specs=in_specs, out_specs=out_specs, check_vma=False)
```

profile of v0, /device:TPU:1, one launch (start us, length us, event | category | flops | bytes accessed | tf_op | source)
XLA Modules:
  0.0 579.5 jit_solution(12865250881409455669)
XLA Ops:
  7.2 0.7 all-gather.8.cloned.1.call-update
  7.9 16.1 %all_gather.25 = bf16[16,8192]{1,0:T(8,128)(2,1)S(1)} all-gather(bf16[16,1024]{1,0:T(8,128)(2,1)} %param.20), channel_id=1, replica_groups=mesh['ctx'=32,'hx'=8] {'hx'}, dimensions={1}, use_global_device_ids=true | all-gather | bytes 294912 | tf_op jit(solution)/shard_map/all_gather | solution.py:99
  24.9 0.8 reshape.166
  25.7 0.8 slice.134
  26.6 0.8 slice.126
  28.1 2.0 gather_fusion
  30.7 1.8 fusion.74
  32.5 1.7 fusion.72
  34.2 3.2 broadcast_select_fusion
  37.4 4.5 all-gather.8.cloned.1.call-done
  41.9 1.8 fusion.89
  44.7 0.9 copy-done.1
  46.2 1.3 fusion.93
  48.7 1.3 fusion.99
  50.4 0.6 convert_reduce_fusion.4
  51.0 1.3 fusion.23
  53.6 1.3 fusion.95
  55.5 0.6 convert_reduce_fusion.5
  56.1 1.3 fusion.25
  58.7 1.3 fusion.97
  60.0 1.4 fusion.27
  61.5 0.7 copy.77
  62.2 9.5 %all-to-all-start = ((f32[1,16,128]{1,0,2:T(1,128)}), f32[1,16,128]{1,0,2:T(1,128)S(1)}, u32[]{:S(2)}, u32[]{:S(2)}) async-start(f32[1,16,128]{1,0,2:T(1,128)} %copy.77), calls=%async_computation | async-start | bytes 131072 | tf_op jit(solution)/shard_map/all_to_all | solution.py:135
  71.8 1.7 convert_reduce_fusion
  73.5 1.6 convert_reduce_fusion.3
  75.1 1.5 convolution_add_fusion.3
  76.6 1.4 convolution_add_fusion
  78.5 1.4 convolution_add_fusion.1
  80.3 1.4 convolution_add_fusion.2
  81.7 0.7 copy.78
  82.4 9.4 %all-to-all-start.1 = ((f32[1,16,128]{1,0,2:T(1,128)}), f32[1,16,128]{1,0,2:T(1,128)S(1)}, u32[]{:S(2)}, u32[]{:S(2)}) async-start(f32[1,16,128]{1,0,2:T(1,128)} %copy.78), calls=%async_computation.1 | async-start | bytes 131072 | tf_op jit(solution)/shard_map/all_to_all | solution.py:136
  91.9 2.5 maximum_bitcast_fusion
  94.4 4.4 copy.83
  98.7 1.8 all-to-all-done.1
  100.5 7.4 %all-to-all-start.2 = ((f32[1,16,128,512]{3,1,0,2:T(8,128)}), f32[1,16,128,512]{3,1,0,2:T(8,128)}, u32[]{:S(2)}, u32[]{:S(2)}) async-start(f32[1,16,128,512]{3,1,0,2:T(8,128)} %copy.83), calls=%async_computation.2 | async-start | bytes 8388608 | tf_op jit(solution)/shard_map/all_to_all | solution.py:137
  108.1 96.2 %all-to-all-done.2 = f32[1,16,128,512]{3,1,0,2:T(8,128)} async-done(((f32[1,16,128,512]{3,1,0,2:T(8,128)}), f32[1,16,128,512]{3,1,0,2:T(8,128)}, u32[]{:S(2)}, u32[]{:S(2)}) %all-to-all-start.2) | async-done | bytes 4194336 | tf_op jit(solution)/shard_map/all_to_all | solution.py:137
  204.3 2.6 multiply_reduce_fusion
  206.8 0.7 copy.84
  207.7 12.8 %all-gather.3 = f32[8,16,4]{1,2,0:T(4,128)S(1)} all-gather(f32[1,16,4]{1,2,0:T(4,128)S(1)} %bitcast.178), channel_id=2, replica_groups=mesh['ctx'=32,'hx'=8] {'hx'}, dimensions={0}, use_global_device_ids=true | all-gather | bytes 2304 | tf_op jit(solution)/shard_map/all_gather | solution.py:24
  220.5 11.3 %all-gather.4 = f32[8,16,4]{1,2,0:T(4,128)S(1)} all-gather(f32[1,16,4]{1,2,0:T(4,128)S(1)} %bitcast.179), channel_id=3, replica_groups=mesh['ctx'=32,'hx'=8] {'hx'}, dimensions={0}, use_global_device_ids=true | all-gather | bytes 2304 | tf_op jit(solution)/shard_map/all_gather | solution.py:24
  232.0 1.0 slice.180
  233.2 2.5 while.14
  235.8 1.6 fusion.21
  237.5 79.6 %all-reduce.5 = bf16[16,7168]{1,0:T(8,128)(2,1)S(1)} all-reduce(f32[16,7168]{1,0:T(8,128)S(1)} %fusion.21), channel_id=1, replica_groups=mesh['ctx'=32,'hx'=8] {'ctx','hx'}, use_global_device_ids=true, to_apply=%region_21.22 | all-reduce | flops 114688 | bytes 688128 | tf_op jit(solution)/shard_map/psum | solution.py:153
  317.3 2.1 fusion.87
  319.4 4.3 fusion.22
  323.8 247.8 %all-reduce.4.cloned.1.call-done = f32[16,7168]{1,0:T(8,128)} async-done(((f32[16,7168]{1,0:T(8,128)}), f32[16,7168]{1,0:T(8,128)}) %all-reduce.4.cloned.1.call-update) | async-done | bytes 458768
  571.6 1.4 fusion.64
  (147 shorter events, 12.6 us)
Async XLA Ops:
  7.2 20.9 %copy-start = (bf16[16,128,512]{2,1,0:T(8,128)(2,1)S(1)}, bf16[16,128,512]{2,1,0:T(8,128)(2,1)}, u32[]{:S(2)}) copy-start(bf16[16,128,512]{2,1,0:T(8,128)(2,1)} %param.23) | copy-start | bytes 6291460
  7.2 20.3 %copy-start.28 = (s32[16]{0:T(128)S(1)}, s32[16]{0:T(128)}, u32[]{:S(2)}) copy-start(s32[16]{0:T(128)} %param.26) | copy-start | bytes 196
  7.2 20.3 %copy-start.17 = (bf16[16,64,128]{2,1,0:T(8,128)(2,1)S(1)}, bf16[16,64,128]{2,1,0:T(8,128)(2,1)}, u32[]{:S(2)}) copy-start(bf16[16,64,128]{2,1,0:T(8,128)(2,1)} %param.24) | copy-start | bytes 786436
  7.2 34.7 %all-gather.8.cloned.1.call-start = ((), (), s32[]{:S(2)}) async-start(), calls=%async_computation.3 | async-start | bytes 2359296 | tf_op jit(solution)/shard_map/all_gather | solution.py:98
  28.1 2.0 copy-start.23
  41.9 2.2 copy-start.3
  41.9 2.8 copy-start.2
  43.7 1.9 copy-start.1
  44.1 2.1 copy-start.16
  52.4 0.9 copy-start.15
  52.4 1.2 copy-start.14
  52.4 1.2 copy-start.27
  57.5 0.9 copy-start.13
  57.5 1.2 copy-start.26
  60.0 13.4 %copy-start.22 = (f32[4,128]{1,0:T(4,128)S(1)}, f32[4,128]{1,0:T(4,128)}, u32[]{:S(2)}) copy-start(f32[4,128]{1,0:T(4,128)} %convert_reduce_fusion.4) | copy-start | bytes 6148
  62.2 20.2 %all-to-all-start = ((f32[1,16,128]{1,0,2:T(1,128)}), f32[1,16,128]{1,0,2:T(1,128)S(1)}, u32[]{:S(2)}, u32[]{:S(2)}) async-start(f32[1,16,128]{1,0,2:T(1,128)} %copy.77), calls=%async_computation | async-start | bytes 131072 | tf_op jit(solution)/shard_map/all_to_all | solution.py:135
  71.8 3.4 copy-start.4
  73.5 3.1 copy-start.5
  76.6 1.5 copy-start.8
  76.6 1.5 copy-start.20
  76.6 1.8 copy-start.21
  76.6 1.9 copy-start.6
  78.0 1.9 copy-start.9
  78.5 1.7 copy-start.7
  79.9 11.9 %copy-start.10 = (f32[4,128,512]{2,1,0:T(8,128)S(1)}, f32[4,128,512]{2,1,0:T(8,128)}, u32[]{:S(2)}) copy-start(f32[4,128,512]{2,1,0:T(8,128)} %convolution_add_fusion.3) | copy-start | bytes 3145732
  82.4 18.1 %all-to-all-start.1 = ((f32[1,16,128]{1,0,2:T(1,128)}), f32[1,16,128]{1,0,2:T(1,128)S(1)}, u32[]{:S(2)}, u32[]{:S(2)}) async-start(f32[1,16,128]{1,0,2:T(1,128)} %copy.78), calls=%async_computation.1 | async-start | bytes 131072 | tf_op jit(solution)/shard_map/all_to_all | solution.py:136
  100.5 103.7 %all-to-all-start.2 = ((f32[1,16,128,512]{3,1,0,2:T(8,128)}), f32[1,16,128,512]{3,1,0,2:T(8,128)}, u32[]{:S(2)}, u32[]{:S(2)}) async-start(f32[1,16,128,512]{3,1,0,2:T(8,128)} %copy.83), calls=%async_computation.2 | async-start | bytes 8388608 | tf_op jit(solution)/shard_map/all_to_all | solution.py:137
  107.9 124.0 %all-gather.10.cloned.1.call-start = ((), (), s32[]{:S(2)}) async-start(), calls=%async_computation.4 | async-start | bytes 1179648 | tf_op jit(solution)/shard_map/all_gather | solution.py:24
  204.3 3.4 copy-start.24
  204.3 3.4 copy-start.25
  207.6 363.9 %all-reduce.4.cloned.1.call-start = ((), (), s32[]{:S(2)}) async-start(), calls=%async_computation.5 | async-start | bytes 917504
  232.0 1.2 slice-start
  233.0 2.9 copy-start.19
  233.2 83.9 %copy-start.12 = (bf16[16,7168]{1,0:T(8,128)(2,1)S(1)}, bf16[16,7168]{1,0:T(8,128)(2,1)}, u32[]{:S(2)}) copy-start(bf16[16,7168]{1,0:T(8,128)(2,1)} %param.29) | copy-start | bytes 688132
  235.7 81.6 %copy-start.18 = (f32[7168]{0:T(1024)S(1)}, f32[7168]{0:T(1024)}, u32[]{:S(2)}) copy-start(f32[7168]{0:T(1024)} %param.30) | copy-start | bytes 86020
  317.1 6.6 %copy-start.11 = (bf16[16,7168]{1,0:T(8,128)(2,1)}, bf16[16,7168]{1,0:T(8,128)(2,1)S(1)}, u32[]{:S(2)}) copy-start(bf16[16,7168]{1,0:T(8,128)(2,1)S(1)} %all-reduce.5) | copy-start | bytes 688132
Sparse Core Ops, SparseCore 0:
  9.9 31.9 all-gather.7
  207.7 24.1 all-gather.9
  323.9 247.6 all-reduce.3
where the time goes:
time: 580 us; the launch traced here: 579 us
  waiting for transfers between devices  351 us (61%)
  blocking collectives  120 us (21%)
  matrix products  27.7 us (5%)
  starting transfers between devices  26.5 us (5%)
  other arithmetic  20.7 us (4%)
  local copies, waits for them, and re-layouts  19.3 us (3%)
  between operations  14.3 us (2%)
    unnamed x4, waiting for transfers between devices  249 us
    all_to_all x1, waiting for transfers between devices, local(): lax.all_to_all(weighted[None], 'ctx', split_axis=2, concat_axis=0, tiled=...  96.2 us
    psum x1, blocking collectives, local(): attended = lax.psum(partial_out, ('ctx', 'hx')).astype(jnp.bfloat16)  79.6 us
    all_gather x2, blocking collectives, merged(): pieces = jax.tree.map(lambda part: lax.all_gather(part, axis), value)  24.1 us
    all_gather x1, blocking collectives, local(): lax.all_gather(query_rope, 'hx', axis=1, tiled=True)  16.1 us
  transfers between devices with their start and end apart: 6, of which 5 were waited for; matrix products, arithmetic and copies ran while one was open for 5% of the time, Pallas kernels for 0%

commit v1 on v0

v1 whole, which is shorter than its diff:
```python
import functools
import math

import jax
import jax.numpy as jnp
from jax import lax
from jax.experimental import pallas as pl
from jax.experimental.pallas import tpu as pltpu
from jax.sharding import PartitionSpec as P

MESH = pl.DeviceIdType.MESH
F32 = jnp.float32
BF16 = jnp.bfloat16

DL = 512
DR = 64
DN = 128
D = 7168
HYPS = 16
HEADS = 128
MSCALE = 1.0 + 0.1 * math.log(40.0)
SCALE = MSCALE * MSCALE / math.sqrt(DN + DR) * math.log2(math.e)
NEG = -1e30
NT = (((1,), (1,)), ((), ()))

N_SEMS = 112
N_LOCAL = 24


def fold(parts):
    top = functools.reduce(jnp.maximum, [p[0] for p in parts])
    total, acc = 0.0, 0.0
    for high, tot, sums in parts:
        factor = jnp.exp2(high - top)
        total = total + tot * factor
        acc = acc + sums * factor
    return top, total, acc


def stat_lanes(columns, rows):
    lane = lax.broadcasted_iota(jnp.int32, (rows, 128), 1)
    out = jnp.zeros((rows, 128), F32)
    for j, column in enumerate(columns):
        out = jnp.where(lane == j, column, out)
    return out


def pack896(part):
    low = jnp.concatenate([part[:, 512:], jnp.zeros((8, 128), part.dtype)], axis=1)
    return jnp.concatenate([part[:, :512], low], axis=0)


def kernel(
    q_hbm, ck_hbm, cr_hbm, sl_hbm, sr_hbm, wuv_hbm, wo_hbm, wg_hbm, wu_hbm, wd_hbm,
    len_ref, par_ref, hid_ref, gain_ref, ids_ref, gw_ref,
    att_ref, upd_ref,
    qv, kv, kr, s0, s1, sr0, sr1, wuv, wo, wg, wu, wd,
    ob, st, xr, xst, ya, yst, yb, ysb, yr, ysr, zt, zsb, zr,
    csb, cr1, c2, c3, c3o, res, nrm, esb, er1, e2f, e2b, er2, e3b, er3,
    ss, rs, ls,
):
    ctx, hx = lax.axis_index("ctx"), lax.axis_index("hx")
    x, z = lax.div(ctx, 8), lax.rem(ctx, 8)
    y, k = lax.div(hx, 2), lax.rem(hx, 2)
    chip = ctx * 4 + y

    def dev(dx=0, dy=0, dz=0, dk=0):
        xx, yy = lax.rem(x + dx, 4), lax.rem(y + dy, 4)
        zz, kk = lax.rem(z + dz, 8), lax.rem(k + dk, 2)
        return (xx * 8 + zz, yy * 2 + kk)

    count = [0, 0]
    sends = []

    def remote(src, dst, where):
        i = count[0]
        count[0] += 1
        copy = pltpu.make_async_remote_copy(
            src_ref=src, dst_ref=dst, send_sem=ss.at[i], recv_sem=rs.at[i],
            device_id=where, device_id_type=MESH,
        )
        copy.start()
        sends.append(copy)
        return copy

    def local(src, dst):
        i = count[1]
        count[1] += 1
        copy = pltpu.make_async_copy(src, dst, ls.at[i])
        copy.start()
        return copy

    kk = 1 - k
    head_rows = pl.ds(pl.multiple_of(hx * 16, 16), 16)
    key_rows = pl.ds(pl.multiple_of(k * 512, 512), 512)
    suf_rows = pl.ds(pl.multiple_of(k * 128, 128), 128)
    uo_rows = pl.ds(pl.multiple_of(k * 64, 64), 64)
    unit_rows = pl.ds(pl.multiple_of(k * 128, 128), 128)
    sv, srv = (s0, s1), (sr0, sr1)

    def kv_pairs(r, core):
        return (
            (ck_hbm.at[2 * core + r], kv.at[r, key_rows]),
            (sl_hbm.at[pl.ds(8 * core + 4 * r, 4)], sv[r].at[:, suf_rows]),
            (cr_hbm.at[2 * core + r], kr.at[r, :, key_rows]),
            (sr_hbm.at[pl.ds(8 * core + 4 * r, 4)], srv[r].at[:, :, suf_rows]),
        )

    w_pairs = (
        (wuv_hbm, wuv.at[k]),
        (wo_hbm, wo.at[uo_rows]),
        (wg_hbm, wg.at[unit_rows]),
        (wu_hbm, wu.at[unit_rows]),
        (wd_hbm, wd.at[unit_rows]),
    )

    HX = [(dy, dk) for dy in (1, 3, 2, 0) for dk in range(2) if dy or dk]
    XY = [(dx, dy) for dx in range(4) for dy in range(4) if dx or dy]

    barrier = pltpu.get_barrier_semaphore()
    peers = [dev(dy=dy, dk=1) for dy in range(4)]
    peers += [dev(dx=dx, dy=dy) for dx, dy in XY]
    peers += [dev(dz=dz) for dz in range(1, 8)]
    for peer in peers:
        pl.semaphore_signal(barrier, inc=1, device_id=peer, device_id_type=MESH)
    own = []
    for r in range(2):
        own.append([local(q_hbm.at[pl.ds(8 * k + 4 * r, 4)], qv.at[pl.ds(4 * r, 4), head_rows])])
        own[r] += [local(src, dst) for src, dst in kv_pairs(r, k)]
    own_w = [local(src, dst) for src, dst in w_pairs]
    pl.semaphore_wait(barrier, len(peers))

    def send_inputs(r):
        got = []
        for dy, dk in HX:
            core = lax.rem(k + dk, 2)
            src = q_hbm.at[pl.ds(8 * core + 4 * r, 4)]
            got.append(remote(src, qv.at[pl.ds(4 * r, 4), head_rows], dev(dy=dy, dk=dk)))
        for src, dst in kv_pairs(r, kk):
            got.append(remote(src, dst, dev(dk=1)))
        return got

    got_in = [send_inputs(0), send_inputs(1)]
    got_w = [remote(src, dst, dev(dk=1)) for src, dst in w_pairs]

    def attend(r):
        for copy in own[r]:
            copy.wait()
        for copy in got_in[r]:
            copy.wait_recv()
        q = qv[4 * r : 4 * r + 4]
        ql = q[..., :DL].reshape(4 * HEADS, DL)
        qr = q[..., DL : DL + DR].reshape(4 * HEADS, DR)
        s = lax.dot_general(ql, kv[r], NT, preferred_element_type=F32)
        s = s + jnp.dot(qr, kr[r], preferred_element_type=F32)
        pos = chip * 1024 + lax.broadcasted_iota(jnp.int32, (1, 1024), 1)
        s = jnp.where(pos < len_ref[2 * k + r], s * SCALE, NEG)
        high = jnp.max(s, axis=1, keepdims=True)
        rows = [slice(i * HEADS, (i + 1) * HEADS) for i in range(4)]
        own_s, tops, parent = [], [], []
        for i in range(4):
            p = lax.rem(par_ref[8 * k + 4 * r + i], 4)
            si = lax.dot_general(q[i, :, :DL], sv[r][p], NT, preferred_element_type=F32)
            si = si + jnp.dot(q[i, :, DL : DL + DR], srv[r][p], preferred_element_type=F32)
            own_s.append(si * SCALE)
            tops.append(jnp.maximum(high[rows[i]], jnp.max(own_s[i], axis=1, keepdims=True)))
            parent.append(p)
        w = jnp.exp2(s - jnp.concatenate(tops, axis=0)).astype(BF16)
        total = jnp.sum(w.astype(F32), axis=1, keepdims=True)
        acc = jnp.dot(w, kv[r], preferred_element_type=F32)
        totals = []
        for i in range(4):
            wi = jnp.exp2(own_s[i] - tops[i]).astype(BF16)
            totals.append(total[rows[i]] + jnp.sum(wi.astype(F32), axis=1, keepdims=True))
            ai = acc[rows[i]] + jnp.dot(wi, sv[r][parent[i]], preferred_element_type=F32)
            ob[4 * r + i] = ai.astype(BF16)
        st[r] = stat_lanes(tops + totals, HEADS)

    def x_send(r):
        got = []
        for dx in (1, 3, 2):
            rows = pl.ds(pl.multiple_of(lax.rem(x + dx, 4) * 32, 32), 32)
            got.append(remote(ob.at[pl.ds(4 * r, 4), rows], xr.at[r, dx - 1], dev(dx=dx)))
            got.append(remote(st.at[r, rows], xst.at[r, dx - 1], dev(dx=dx)))
        return got

    def x_sum(r, got):
        for copy in got:
            copy.wait_recv()
        rows = pl.ds(pl.multiple_of(x * 32, 32), 32)
        stats = [st[r, rows]] + [xst[r, j] for j in range(3)]
        tops, totals = [], []
        for i in range(4):
            sums = [ob[4 * r + i, rows]] + [xr[r, j, i] for j in range(3)]
            parts = [
                (t[:, i : i + 1], t[:, 4 + i : 5 + i], a.astype(F32))
                for t, a in zip(stats, sums)
            ]
            top, total, acc = fold(parts)
            for l in range(4):
                ya[r, i, l] = acc[:, 128 * l : 128 * l + 128]
            tops.append(top)
            totals.append(total)
        yst[r] = stat_lanes(tops + totals, 32)
        for d in range(4):
            pick = pl.ds(d, 8, stride=4)
            for l in range(4):
                block = jnp.concatenate([ya[r, i, l, pick, :] for i in range(4)], axis=0)
                yb[r, d, :, 128 * l : 128 * l + 128] = block.astype(BF16)
            ysb[r, d] = yst[r, pick, :]

    def y_send(r):
        got = []
        for dy in (1, 3, 2):
            to = lax.rem(y + dy, 4)
            got.append(remote(yb.at[r, to], yr.at[r, dy - 1], dev(dy=dy)))
            got.append(remote(ysb.at[r, to], ysr.at[r, dy - 1], dev(dy=dy)))
        return got

    def y_sum(r, got):
        for copy in got:
            copy.wait_recv()
        stats = [ysb[r, y]] + [ysr[r, j] for j in range(3)]
        sums = [yb[r, y].astype(F32)] + [yr[r, j].astype(F32) for j in range(3)]
        for i in range(4):
            parts = [
                (t[:, i : i + 1], t[:, 4 + i : 5 + i], a[8 * i : 8 * i + 8])
                for t, a in zip(stats, sums)
            ]
            top, total, acc = fold(parts)
            at = pl.ds((4 * r + i) * 8, 8)
            for l in range(4):
                zt[l, at] = acc[:, 128 * l : 128 * l + 128]
            zt[4, at] = stat_lanes([top, total], 8)

    attend(0)
    got_x0 = x_send(0)
    attend(1)
    got_x1 = x_send(1)
    x_sum(0, got_x0)
    got_y0 = y_send(0)
    x_sum(1, got_x1)
    got_y1 = y_send(1)
    y_sum(0, got_y0)
    y_sum(1, got_y1)
    for b in range(8):
        for l in range(5):
            zsb[b, :, 128 * l : 128 * l + 128] = zt[l, pl.ds(b, 8, stride=8), :]
    got = []
    for dz in (4, 3, 5, 2, 6, 1, 7):
        got.append(remote(zsb.at[lax.rem(z + dz, 8)], zr.at[dz - 1], dev(dz=dz)))
    for copy in got:
        copy.wait_recv()
    parts = []
    for a in [zsb[z]] + [zr[j] for j in range(7)]:
        parts.append((a[:, DL : DL + 1], a[:, DL + 1 : DL + 2], a[:, :DL]))
    top, total, acc = fold(parts)
    attention = (acc / total).astype(BF16)

    for copy in own_w[:2]:
        copy.wait()
    for copy in got_w[:2]:
        copy.wait_recv()
    v0 = jnp.dot(attention, wuv[0], preferred_element_type=F32).astype(BF16)
    v1 = jnp.dot(attention, wuv[1], preferred_element_type=F32).astype(BF16)
    for b in range(8):
        cols = slice(896 * b, 896 * b + 896)
        term = jnp.dot(v0, wo[:64, cols], preferred_element_type=F32)
        term = term + jnp.dot(v1, wo[64:, cols], preferred_element_type=F32)
        csb[b] = pack896(term).astype(BF16)
    got = []
    for dz in (4, 3, 5, 2, 6, 1, 7):
        got.append(remote(csb.at[lax.rem(z + dz, 8)], cr1.at[dz - 1], dev(dz=dz)))
    for copy in got:
        copy.wait_recv()
    part = csb[z].astype(F32)
    for j in range(7):
        part = part + cr1[j].astype(F32)
    me = x * 4 + y
    c2[me] = part.astype(BF16)
    got = []
    for dx, dy in sorted(XY, key=lambda d: -(min(d[0], 4 - d[0]) + min(d[1], 4 - d[1]))):
        got.append(remote(c2.at[me], c2.at[me], dev(dx=dx, dy=dy)))
    for copy in got:
        copy.wait_recv()
    part = c2[0].astype(F32)
    for j in range(1, 16):
        part = part + c2[j].astype(F32)
    c3[z] = part.astype(BF16)
    got = []
    for dz in (4, 3, 5, 2, 6, 1, 7):
        got.append(remote(c3.at[z], c3.at[z], dev(dz=dz)))
    for copy in got:
        copy.wait_recv()
    got_att = remote(c3, c3o, dev(dk=1))

    square = jnp.zeros((8, 1), F32)
    for b in range(8):
        block = c3[b].astype(F32)
        for half, width in ((0, 512), (1, 384)):
            cols = slice(896 * b + 512 * half, 896 * b + 512 * half + width)
            hid = hid_ref[:, cols].astype(F32)
            hid = jnp.where(k == 0, hid[:8], hid[8:])
            value = hid + block[8 * half : 8 * half + 8, :width]
            res[:, cols] = value
            square = square + jnp.sum(value * value, axis=1, keepdims=True)
    scale = lax.rsqrt(square / D + 1e-6)
    nrm[...] = (res[...] * scale * gain_ref[...]).astype(BF16)

    expert = lax.div(ctx, 2)
    route = jnp.sum(gw_ref[...] * (ids_ref[...] == expert).astype(F32), axis=1, keepdims=True)
    route = jnp.where(k == 0, route[:8], route[8:])
    for copy in own_w[2:]:
        copy.wait()
    for copy in got_w[2:]:
        copy.wait_recv()
    gate = lax.dot_general(nrm[...], wg[...], NT, preferred_element_type=F32)
    up = lax.dot_general(nrm[...], wu[...], NT, preferred_element_type=F32)
    act = (gate / (1.0 + jnp.exp(-gate)) * up * route).astype(BF16)
    for b in range(4):
        cols = slice(1792 * b, 1792 * b + 1792)
        term = jnp.dot(act, wd[:, cols], preferred_element_type=F32)
        esb[b] = jnp.concatenate([term[:, :896], term[:, 896:]], axis=0).astype(BF16)
    got = []
    for dx in (2, 1, 3):
        got.append(remote(esb.at[lax.rem(x + dx, 4)], er1.at[dx - 1], dev(dx=dx)))
    for copy in got:
        copy.wait_recv()
    part = esb[x].astype(F32)
    for j in range(3):
        part = part + er1[j].astype(F32)
    part = jnp.concatenate([part[:8], part[8:]], axis=1)
    lane = lax.broadcasted_iota(jnp.int32, (8, 1792), 1)
    mine = (lane >= z * 224) & (lane < z * 224 + 224) & (y == 0)
    rest = res[:, pl.ds(pl.multiple_of(x * 1792, 128), 1792)]
    part = part + jnp.where(mine, rest, 0.0)
    for b in range(8):
        piece = part[:, 224 * b : 224 * b + 224]
        piece = jnp.concatenate([piece, jnp.zeros((8, 32), F32)], axis=1)
        e2f[b] = piece
        e2b[b] = jnp.concatenate([piece[:, :128], piece[:, 128:]], axis=0).astype(BF16)
    got = []
    for dz in (4, 3, 5, 2, 6, 1, 7):
        got.append(remote(e2b.at[lax.rem(z + dz, 8)], er2.at[dz - 1], dev(dz=dz)))
    for copy in got:
        copy.wait_recv()
    part = er2[0].astype(F32)
    for j in range(1, 7):
        part = part + er2[j].astype(F32)
    part = jnp.concatenate([part[:8], part[8:]], axis=1) + e2f[z]
    for b in range(8):
        piece = part[:, 28 * b : 28 * b + 28]
        e3b[b] = jnp.concatenate([piece, jnp.zeros((8, 100), F32)], axis=1)
    got = []
    for dy, dk in HX:
        to = lax.rem(y + dy, 4) * 2 + lax.rem(k + dk, 2)
        got.append(remote(e3b.at[to], er3.at[2 * dy + dk], dev(dy=dy, dk=dk)))
    for copy in got:
        copy.wait_recv()
    same = e3b[hx] + er3[2] + er3[4] + er3[6]
    other = er3[1] + er3[3] + er3[5] + er3[7]
    both = jnp.concatenate(
        [jnp.where(k == 0, same, other), jnp.where(k == 0, other, same)], axis=0
    )
    upd_ref[...] = both[:, :28].astype(BF16)

    got_att.wait_recv()
    for b in range(8):
        a, o = c3[b].astype(F32), c3o[b].astype(F32)
        first, second = jnp.where(k == 0, a, o), jnp.where(k == 0, o, a)
        for half, width in ((0, 512), (1, 384)):
            cols = slice(896 * b + 512 * half, 896 * b + 512 * half + width)
            rows = slice(8 * half, 8 * half + 8)
            pair = jnp.concatenate([first[rows, :width], second[rows, :width]], axis=0)
            att_ref[:, cols] = pair.astype(BF16)
    for copy in sends:
        copy.wait_send()


def local(
    query_latent, query_rope, cache_latent, cache_rope, suffix_latent, suffix_rope, lengths,
    parents, w_uv, w_o, hidden, norm_gain, w_gate, w_up, w_down, expert_ids, gate_weights,
):
    q = jnp.concatenate([query_latent, query_rope.reshape(HYPS, 16, DR)], axis=2)
    hbm = pl.BlockSpec(memory_space=pl.ANY)
    vmem = pl.BlockSpec(memory_space=pltpu.VMEM)
    smem = pl.BlockSpec(memory_space=pltpu.SMEM)
    scratch = [
        ((8, 128, DL + DR), BF16),
        ((2, 1024, DL), BF16),
        ((2, DR, 1024), BF16),
        ((4, 256, DL), BF16),
        ((4, 256, DL), BF16),
        ((4, DR, 256), BF16),
        ((4, DR, 256), BF16),
        ((2, DL, 64), BF16),
        ((128, D), BF16),
        ((256, D), BF16),
        ((256, D), BF16),
        ((256, D), BF16),
        ((8, 128, DL), BF16),
        ((2, 128, 128), F32),
        ((2, 3, 4, 32, DL), BF16),
        ((2, 3, 32, 128), F32),
        ((2, 4, 4, 32, 128), F32),
        ((2, 32, 128), F32),
        ((2, 4, 32, DL), BF16),
        ((2, 4, 8, 128), F32),
        ((2, 3, 32, DL), BF16),
        ((2, 3, 8, 128), F32),
        ((5, 64, 128), F32),
        ((8, 8, 640), F32),
        ((7, 8, 640), F32),
        ((8, 16, 512), BF16),
        ((7, 16, 512), BF16),
        ((16, 16, 512), BF16),
        ((8, 16, 512), BF16),
        ((8, 16, 512), BF16),
        ((8, D), F32),
        ((8, D), BF16),
        ((4, 16, 896), BF16),
        ((3, 16, 896), BF16),
        ((8, 8, 256), F32),
        ((8, 16, 128), BF16),
        ((7, 16, 128), BF16),
        ((8, 8, 128), F32),
        ((8, 8, 128), F32),
    ]
    return pl.pallas_call(
        kernel,
        name="decode_step",
        out_shape=(
            jax.ShapeDtypeStruct((HYPS, D), BF16),
            jax.ShapeDtypeStruct((HYPS, 28), BF16),
        ),
        in_specs=[hbm] * 10 + [smem] * 2 + [vmem] * 4,
        out_specs=(vmem, vmem),
        scratch_shapes=[pltpu.VMEM(shape, dtype) for shape, dtype in scratch]
        + [
            pltpu.SemaphoreType.DMA((N_SEMS,)),
            pltpu.SemaphoreType.DMA((N_SEMS,)),
            pltpu.SemaphoreType.DMA((N_LOCAL,)),
        ],
        compiler_params=pltpu.CompilerParams(
            collective_id=0, has_side_effects=True, vmem_limit_bytes=48 << 20
        ),
    )(
        q, cache_latent, cache_rope, suffix_latent, suffix_rope, w_uv, w_o, w_gate, w_up, w_down,
        lengths, parents, hidden, norm_gain.reshape(1, D), expert_ids, gate_weights,
    )


def solution(mesh):
    both = ("ctx", "hx")
    in_specs = (
        P(None, "hx", None),
        P(None, "hx"),
        P(None, both, None),
        P(None, None, both),
        P(None, both, None),
        P(None, None, both),
        P(),
        P(),
        P(None, both),
        P(both, None),
        P(),
        P(),
        P(both, None),
        P(both, None),
        P(both, None),
        P(),
        P(),
    )
    out_specs = (P(), P(None, both))
    return jax.shard_map(local, mesh=mesh, in_specs=in_specs, out_specs=out_specs, check_vma=False)
```

time: 580 us -> 97.7 us (0.17)
  waiting for transfers between devices: 351 us -> 0 us
  blocking collectives: 120 us -> 0 us
  Pallas kernels: 0 us -> 81.8 us
  matrix products: 27.7 us -> 0 us
  starting transfers between devices: 26.5 us -> 0 us
  other arithmetic: 20.7 us -> 0.98 us
  between operations: 14.3 us -> 0.67 us
    unnamed x4 -> x0, waiting for transfers between devices: 249 us -> none
    all_to_all x3 -> x0, waiting for transfers between devices: 98 us -> none  [the longest x1 96.2 us: local(): lax.all_to_all(weighted[None], 'ctx', split_axis=2, concat_axis=0, tiled=...]
    pallas_call x0 -> x1, Pallas kernels: none -> 81.8 us  [local(): pl.pallas_call(kernel, name='decode_step', out_shape=(jax.ShapeDtypeStruc...]
    psum x1 -> x0, blocking collectives: 79.6 us -> none  [local(): attended = lax.psum(partial_out, ('ctx', 'hx')).astype(jnp.bfloat16)]
    all_gather x3 -> x0, blocking collectives: 40.2 us -> none  [the longest x2 24.1 us: merged(): pieces = jax.tree.map(lambda part: lax.all_gather(part, axis), value)]
    dot_general x27 -> x0, matrix products: 27.7 us -> none  [the longest x4 5.74 us: request_stats(): jnp.dot(pre_weights.reshape(beam_count * head_count, -1), pre_lat, prefer...]
    all_to_all x3 -> x0, starting transfers between devices: 26.3 us -> none  [the longest x1 9.54 us: local(): lax.all_to_all(row_max[None], 'ctx', split_axis=2, concat_axis=0, tiled=T...]
    unnamed x58 -> x23, local copies, waits for them, and re-layouts: 1.93 us -> 12.8 us
  transfers between devices with their start and end apart: 6 -> 0, of which waited for: 5 -> 0; matrix products, arithmetic and copies ran while one was open for 5% -> 0% of each run, Pallas kernels for 0% -> 0%
where the time goes in v1:
time: 97.7 us; the launch traced here: 97.1 us
  Pallas kernels  81.8 us (84%)
  local copies, waits for them, and re-layouts  13.7 us (14%)
  other arithmetic  0.98 us (1%)
    pallas_call x1, Pallas kernels, local(): pl.pallas_call(kernel, name='decode_step', out_shape=(jax.ShapeDtypeStruc...  81.8 us
    unnamed x23, local copies, waits for them, and re-layouts  12.8 us

profile of v1, /device:TPU:1, one launch (start us, length us, event | category | flops | bytes accessed | tf_op | source)
XLA Modules:
  0.0 97.1 jit_solution(13997835815690002133)
XLA Ops:
  0.6 0.8 copy.20.ids_ref
  1.4 0.8 copy.21.gw_ref
  2.1 0.9 reshape.10
  3.0 1.0 copy.19.wuv_hbm
  4.0 1.0 %pad_maximum_fusion.q_hbm = bf16[16,16,576]{2,1,0:T(8,128)(2,1)S(1)} fusion(bf16[16,16,64]{2,1,0:T(8,128)(2,1)S(1)} %reshape.10, bf16[16,16,512]{2,1,0:T(8,128)(2,1)} %param.17), kind=kLoop, calls=%fused_computation | loop fusion | flops 589824 | bytes 589824 | tf_op jit(solution)/shard_map/concatenate | solution.py:384
  5.0 0.0 copy-start
  5.0 1.5 %copy-done = bf16[128,7168]{1,0:T(8,128)(2,1)S(1)} copy-done((bf16[128,7168]{1,0:T(8,128)(2,1)S(1)}, bf16[128,7168]{1,0:T(8,128)(2,1)}, u32[]{:S(2)}) %copy-start) | copy-done | bytes 1835032
  6.5 0.0 copy-start.1
  6.5 1.5 %copy-done.1 = bf16[128,7168]{1,0:T(8,128)(2,1)S(1)} copy-done((bf16[128,7168]{1,0:T(8,128)(2,1)S(1)}, bf16[128,7168]{1,0:T(8,128)(2,1)}, u32[]{:S(2)}) %copy-start.1) | copy-done | bytes 1835032
  8.0 0.0 copy-start.2
  8.0 1.2 %copy-done.2 = bf16[64,7168]{1,0:T(8,128)(2,1)S(1)} copy-done((bf16[64,7168]{1,0:T(8,128)(2,1)S(1)}, bf16[64,7168]{1,0:T(8,128)(2,1)}, u32[]{:S(2)}) %copy-start.2) | copy-done | bytes 917528
  9.2 0.0 copy-start.3
  9.2 0.9 copy-done.3
  10.1 0.0 copy-start.4
  10.1 0.9 copy-done.4
  11.1 0.0 copy-start.5
  11.1 0.9 copy-done.5
  12.0 0.0 copy-start.6
  12.0 0.7 copy-done.6
  12.7 0.0 copy-start.7
  12.7 0.7 copy-done.7
  13.4 0.0 copy-start.8
  13.4 0.7 copy-done.8
  14.1 81.8 %decode_step.1 = (bf16[16,7168]{1,0:T(8,128)(2,1)S(1)}, bf16[16,28]{1,0:T(8,128)(2,1)S(1)}) custom-call(bf16[16,16,576]{2,1,0:T(8,128)(2,1)S(1)} %pad_maximum_fusion.q_hbm, bf16[4,512,512]{2,1,0:T(8,128)(2,1)} %ck_hbm.1, bf16[4,64,512]{2,1,0:T(8,128)(2,1)S(1)} %copy-done.3, bf16[16,128,512]{2,1,0:T(8,128)(2,1)} %sl_hbm.1, ...), custom_call_target="tpu_custom_call" | custom-call | tf_op jit(solution)/shard_map/decode_step/pallas_call | solution.py:429
  95.8 0.7 copy.24
  96.5 0.6 copy.25
Async XLA Ops:
  5.0 1.5 %copy-start = (bf16[128,7168]{1,0:T(8,128)(2,1)S(1)}, bf16[128,7168]{1,0:T(8,128)(2,1)}, u32[]{:S(2)}) copy-start(bf16[128,7168]{1,0:T(8,128)(2,1)} %wg_hbm.1) | copy-start | bytes 5505028
  6.5 1.5 %copy-start.1 = (bf16[128,7168]{1,0:T(8,128)(2,1)S(1)}, bf16[128,7168]{1,0:T(8,128)(2,1)}, u32[]{:S(2)}) copy-start(bf16[128,7168]{1,0:T(8,128)(2,1)} %wu_hbm.1) | copy-start | bytes 5505028
  8.0 1.2 %copy-start.2 = (bf16[64,7168]{1,0:T(8,128)(2,1)S(1)}, bf16[64,7168]{1,0:T(8,128)(2,1)}, u32[]{:S(2)}) copy-start(bf16[64,7168]{1,0:T(8,128)(2,1)} %wo_hbm.1) | copy-start | bytes 2752516
  9.2 0.9 copy-start.3
  10.1 0.9 copy-start.4
  11.1 0.9 copy-start.5
  12.0 0.7 copy-start.6
  12.7 0.7 copy-start.7
  13.4 0.7 copy-start.8

commit v2 on v1

v2 whole, which is shorter than its diff:
```python
import functools
import math

import jax
import jax.numpy as jnp
from jax import lax
from jax.experimental import pallas as pl
from jax.experimental.pallas import tpu as pltpu
from jax.sharding import PartitionSpec as P

MESH = pl.DeviceIdType.MESH
F32 = jnp.float32
BF16 = jnp.bfloat16

DL = 512
DR = 64
DN = 128
D = 7168
HYPS = 16
HEADS = 128
MSCALE = 1.0 + 0.1 * math.log(40.0)
SCALE = MSCALE * MSCALE / math.sqrt(DN + DR) * math.log2(math.e)
NEG = -1e30
NT = (((1,), (1,)), ((), ()))

N_SEMS = 168
N_LOCAL = 24


def fold(parts):
    top = functools.reduce(jnp.maximum, [p[0] for p in parts])
    total, acc = 0.0, 0.0
    for high, tot, sums in parts:
        factor = jnp.exp2(high - top)
        total = total + tot * factor
        acc = acc + sums * factor
    return top, total, acc


def stat_lanes(columns, rows):
    lane = lax.broadcasted_iota(jnp.int32, (rows, 128), 1)
    out = jnp.zeros((rows, 128), F32)
    for j, column in enumerate(columns):
        out = jnp.where(lane == j, column, out)
    return out


def window(tiles, start, dest):
    at, off = divmod(start, 128)
    shift = (dest - off) % 128
    out = pltpu.roll(tiles[at], shift, 1) if shift else tiles[at]
    if off + 56 > 128:
        lane = lax.broadcasted_iota(jnp.int32, (8, 128), 1)
        after = pltpu.roll(tiles[at + 1], shift, 1) if shift else tiles[at + 1]
        out = jnp.where(lane < dest + 128 - off, out, after)
    return out


def pack896(part):
    low = jnp.concatenate([part[:, 512:], jnp.zeros((8, 128), part.dtype)], axis=1)
    return jnp.concatenate([part[:, :512], low], axis=0)


def kernel(
    ql_hbm, qr_hbm, ck_hbm, cr_hbm, sl_hbm, sr_hbm, wuv_hbm, wo_hbm, wg_hbm, wu_hbm, wd_hbm,
    len_hbm, par_hbm, hid_hbm, gain_hbm, ids_hbm, gw_hbm,
    att_ref, upd_ref,
    hid_ref, gain_ref, ids_ref, gw_ref, rope, ropes, qc, qv0, qv1, kv, kr, s0, s1, sr0, sr1,
    wuv, wo, wg, wu, wd, tmp, st, ob, osb, br, bsr, zt, zsb, zr,
    csb, cr1, c2, c3, c3o, res, nrm, e1f, esb, er1, e2b, er2,
    len_ref, par_ref, ss, rs, ls,
):
    ctx, hx = lax.axis_index("ctx"), lax.axis_index("hx")
    x, z = lax.div(ctx, 8), lax.rem(ctx, 8)
    y, k = lax.div(hx, 2), lax.rem(hx, 2)
    chip = ctx * 4 + y

    def dev(dx=0, dy=0, dz=0, dk=0):
        xx, yy = lax.rem(x + dx, 4), lax.rem(y + dy, 4)
        zz, kk = lax.rem(z + dz, 8), lax.rem(k + dk, 2)
        return (xx * 8 + zz, yy * 2 + kk)

    count = [0, 0]
    sends = []

    def remote(src, dst, where):
        i = count[0]
        count[0] += 1
        copy = pltpu.make_async_remote_copy(
            src_ref=src, dst_ref=dst, send_sem=ss.at[i], recv_sem=rs.at[i],
            device_id=where, device_id_type=MESH,
        )
        copy.start()
        sends.append(copy)
        return copy

    def local(src, dst):
        i = count[1]
        count[1] += 1
        copy = pltpu.make_async_copy(src, dst, ls.at[i])
        copy.start()
        return copy

    kk = 1 - k
    head_rows = pl.ds(pl.multiple_of(hx * 16, 16), 16)
    key_rows = pl.ds(pl.multiple_of(k * 512, 512), 512)
    suf_rows = pl.ds(pl.multiple_of(k * 128, 128), 128)
    uo_rows = pl.ds(pl.multiple_of(k * 64, 64), 64)
    unit_rows = pl.ds(pl.multiple_of(k * 128, 128), 128)
    sv, srv = (s0, s1), (sr0, sr1)

    def kv_pairs(r, core):
        rows = slice(DR * r, DR * r + DR)
        return (
            (ck_hbm.at[2 * core + r], kv.at[r, key_rows]),
            (sl_hbm.at[pl.ds(8 * core + 4 * r, 4)], sv[r].at[:, suf_rows]),
            (cr_hbm.at[2 * core + r], kr.at[r, rows, key_rows]),
            (sr_hbm.at[pl.ds(8 * core + 4 * r, 4)], srv[r].at[:, rows, suf_rows]),
        )

    w_pairs = (
        (wuv_hbm, wuv.at[k]),
        (wo_hbm, wo.at[uo_rows]),
        (wg_hbm, wg.at[unit_rows]),
        (wu_hbm, wu.at[unit_rows]),
        (wd_hbm, wd.at[unit_rows]),
    )

    HX = [(dy, dk) for dy in (1, 3, 2, 0) for dk in range(2) if dy or dk]
    XY = [(dx, dy) for dx in range(4) for dy in range(4) if dx or dy]
    XY.sort(key=lambda d: -min(d[0], 4 - d[0]) - min(d[1], 4 - d[1]))
    ZK = [(dz, dk) for dz in (4, 3, 5, 2, 6, 1, 7, 0) for dk in range(2) if dz or dk]

    barrier = pltpu.get_barrier_semaphore()
    peers = [dev(dz=dz, dk=dk) for dz, dk in ZK]
    peers += [dev(dx=dx, dy=dy) for dx, dy in XY]
    peers += [dev(dy=dy, dk=1) for dy in range(1, 4)]
    for peer in peers:
        pl.semaphore_signal(barrier, inc=1, device_id=peer, device_id_type=MESH)
    own_q = [local(qr_hbm, rope)]
    own_q += [local(ql_hbm.at[pl.ds(8 * c, 4)], qc.at[c, :, :, :DL]) for c in range(2)]
    own = [[local(src, dst) for src, dst in kv_pairs(r, k)] for r in range(2)]
    own[0] += [local(len_hbm, len_ref), local(par_hbm, par_ref)]
    own[1].append(local(ql_hbm.at[pl.ds(8 * k + 4, 4)], qv1.at[:, head_rows]))
    own_w = [local(src, dst) for src, dst in w_pairs]
    small = [(hid_hbm, hid_ref), (gain_hbm, gain_ref), (ids_hbm, ids_ref), (gw_hbm, gw_ref)]
    own_small = [local(src, dst) for src, dst in small]
    kr[0, DR:] = jnp.zeros((DR, 1024), BF16)
    kr[1, :DR] = jnp.zeros((DR, 1024), BF16)
    sr0[:, DR:] = jnp.zeros((4, DR, 256), BF16)
    sr1[:, :DR] = jnp.zeros((4, DR, 256), BF16)
    own_q[0].wait()
    low = lax.broadcasted_iota(jnp.int32, (16, 128), 1) < DR
    for t in range(8):
        pair = rope[:, 128 * t : 128 * t + 128].astype(F32)
        swap = pltpu.roll(pair, DR, 1)
        ropes[pl.ds(2 * t, 16, stride=16), :] = jnp.where(low, pair, pltpu.roll(swap, 12, 0))
        ropes[pl.ds(2 * t + 1, 16, stride=16), :] = jnp.where(low, swap, pltpu.roll(pair, 12, 0))
    for c in range(2):
        for i in range(4):
            row = 16 * (8 * c + i)
            qc[c, i, :, DL:] = ropes[row : row + 16, :].astype(BF16)
    own_q[1].wait()
    own_q[2].wait()
    own[0].append(local(qc.at[k], qv0.at[:, head_rows]))
    pl.semaphore_wait(barrier, len(peers))

    beam = lax.rem(x + 2 * z, 4)
    got_q = {}
    for dy, dk in HX:
        core = lax.rem(k + dk, 2)
        if dy:
            src, dst = qc.at[core, beam], qv0.at[beam, head_rows]
        else:
            src, dst = qc.at[core], qv0.at[:, head_rows]
        got_q[dy, dk] = remote(src, dst, dev(dy=dy, dk=dk))
    got_in = [[got_q[0, 1]], []]
    for src, dst in kv_pairs(0, kk):
        got_in[0].append(remote(src, dst, dev(dk=1)))
    for dy in (1, 3, 2):
        for copy in (got_q[dy, 0], got_q[dy, 1]):
            copy.wait_recv()
        rows = pl.ds(pl.multiple_of(lax.rem(y + 4 - dy, 4) * 32, 32), 32)
        block = qv0.at[beam, rows]
        for where in (dev(dx=1), dev(dx=3), dev(dz=1)):
            got_in[0].append(remote(block, block, where))

    for dy, dk in HX:
        core = lax.rem(k + dk, 2)
        src = ql_hbm.at[pl.ds(8 * core + 4, 4)]
        got_in[1].append(remote(src, qv1.at[:, head_rows], dev(dy=dy, dk=dk)))
    for src, dst in kv_pairs(1, kk):
        got_in[1].append(remote(src, dst, dev(dk=1)))
    def attend(r):
        for copy in own[r]:
            copy.wait()
        for copy in got_in[r]:
            copy.wait_recv()
        q = qv0[..., :DL] if r == 0 else qv1[...]
        qr = qv0[..., DL:]
        ql = q.reshape(4 * HEADS, DL)
        s = lax.dot_general(ql, kv[r], NT, preferred_element_type=F32)
        s = s + jnp.dot(
            qr.reshape(4 * HEADS, 128), kr[r], preferred_element_type=F32
        )
        pos = chip * 1024 + lax.broadcasted_iota(jnp.int32, (1, 1024), 1)
        s = jnp.where(pos < len_ref[2 * k + r], s * SCALE, NEG)
        high = jnp.max(s, axis=1, keepdims=True)
        rows = [slice(i * HEADS, (i + 1) * HEADS) for i in range(4)]
        own_s, tops, parent = [], [], []
        for i in range(4):
            p = lax.rem(par_ref[8 * k + 4 * r + i], 4)
            si = lax.dot_general(q[i], sv[r][p], NT, preferred_element_type=F32)
            si = si + jnp.dot(qr[i], srv[r][p], preferred_element_type=F32)
            own_s.append(si * SCALE)
            tops.append(jnp.maximum(high[rows[i]], jnp.max(own_s[i], axis=1, keepdims=True)))
            parent.append(p)
        w = jnp.exp2(s - jnp.concatenate(tops, axis=0)).astype(BF16)
        total = jnp.sum(w.astype(F32), axis=1, keepdims=True)
        acc = jnp.dot(w, kv[r], preferred_element_type=F32)
        totals = []
        for i in range(4):
            wi = jnp.exp2(own_s[i] - tops[i]).astype(BF16)
            totals.append(total[rows[i]] + jnp.sum(wi.astype(F32), axis=1, keepdims=True))
            ai = acc[rows[i]] + jnp.dot(wi, sv[r][parent[i]], preferred_element_type=F32)
            for l in range(4):
                tmp[i, l] = ai[:, 128 * l : 128 * l + 128]
        st[...] = stat_lanes(tops + totals, HEADS)
        for to in range(16):
            pick = pl.ds(32 * (to // 4) + to % 4, 8, stride=4)
            for l in range(4):
                block = jnp.concatenate([tmp[i, l, pick, :] for i in range(4)], axis=0)
                ob[r, to, :, 128 * l : 128 * l + 128] = block.astype(BF16)
            osb[r, to] = st[pick, :]

    me = x * 4 + y

    def join_send(r):
        got = []
        for j, (dx, dy) in enumerate(XY):
            to = lax.rem(x + dx, 4) * 4 + lax.rem(y + dy, 4)
            got.append(remote(osb.at[r, to], bsr.at[r, j], dev(dx=dx, dy=dy)))
            got.append(remote(ob.at[r, to], br.at[r, j], dev(dx=dx, dy=dy)))
        return got

    def join(r, got):
        for copy in got:
            copy.wait_recv()
        stats = [osb[r, me]] + [bsr[r, j] for j in range(15)]
        top = functools.reduce(jnp.maximum, stats)
        factors = [jnp.exp2(stat - top) for stat in stats]
        total = sum(pltpu.roll(f, 4, 1) * stat for f, stat in zip(factors, stats))
        for i in range(4):
            acc = jnp.zeros((8, DL), F32)
            for j in range(16):
                block = ob[r, me] if j == 0 else br[r, j - 1]
                rows = block.astype(F32)[8 * i : 8 * i + 8]
                acc = acc + rows * factors[j][:, i : i + 1]
            at = pl.ds((4 * r + i) * 8, 8)
            for l in range(4):
                zt[l, at] = acc[:, 128 * l : 128 * l + 128]
            zt[4, at] = stat_lanes([top[:, i : i + 1], total[:, 4 + i : 5 + i]], 8)

    attend(0)
    got_b0 = join_send(0)
    got_w = [remote(src, dst, dev(dk=1)) for src, dst in w_pairs]
    attend(1)
    got_b1 = join_send(1)
    join(0, got_b0)
    join(1, got_b1)
    for b in range(8):
        for l in range(5):
            zsb[b, :, 128 * l : 128 * l + 128] = zt[l, pl.ds(b, 8, stride=8), :]
    got = []
    for dz in (4, 3, 5, 2, 6, 1, 7):
        got.append(remote(zsb.at[lax.rem(z + dz, 8)], zr.at[dz - 1], dev(dz=dz)))
    for copy in got:
        copy.wait_recv()
    parts = []
    for a in [zsb[z]] + [zr[j] for j in range(7)]:
        parts.append((a[:, DL : DL + 1], a[:, DL + 1 : DL + 2], a[:, :DL]))
    top, total, acc = fold(parts)
    attention = (acc / total).astype(BF16)

    for copy in own_w[:2]:
        copy.wait()
    for copy in got_w[:2]:
        copy.wait_recv()
    v0 = lax.dot_general(attention, wuv[0], NT, preferred_element_type=F32).astype(BF16)
    v1 = lax.dot_general(attention, wuv[1], NT, preferred_element_type=F32).astype(BF16)
    for b in range(8):
        cols = slice(896 * b, 896 * b + 896)
        term = jnp.dot(v0, wo[:64, cols], preferred_element_type=F32)
        term = term + jnp.dot(v1, wo[64:, cols], preferred_element_type=F32)
        csb[b] = pack896(term).astype(BF16)
    got = []
    for dz in (4, 3, 5, 2, 6, 1, 7):
        got.append(remote(csb.at[lax.rem(z + dz, 8)], cr1.at[dz - 1], dev(dz=dz)))
    for copy in got:
        copy.wait_recv()
    part = csb[z].astype(F32)
    for j in range(7):
        part = part + cr1[j].astype(F32)
    c2[me] = part.astype(BF16)
    got = []
    for dx, dy in XY:
        got.append(remote(c2.at[me], c2.at[me], dev(dx=dx, dy=dy)))
    for copy in got:
        copy.wait_recv()
    part = c2[0].astype(F32)
    for j in range(1, 16):
        part = part + c2[j].astype(F32)
    c3[z] = part.astype(BF16)
    got = []
    for dz in (4, 3, 5, 2, 6, 1, 7):
        got.append(remote(c3.at[z], c3.at[z], dev(dz=dz)))
    for copy in got:
        copy.wait_recv()
    got_att = remote(c3, c3o, dev(dk=1))

    for copy in own_small:
        copy.wait()
    square = jnp.zeros((8, 1), F32)
    for b in range(8):
        block = c3[b].astype(F32)
        for half, width in ((0, 512), (1, 384)):
            cols = slice(896 * b + 512 * half, 896 * b + 512 * half + width)
            hid = hid_ref[:, cols].astype(F32)
            hid = jnp.where(k == 0, hid[:8], hid[8:])
            value = hid + block[8 * half : 8 * half + 8, :width]
            res[:, cols] = value
            square = square + jnp.sum(value * value, axis=1, keepdims=True)
    scale = lax.rsqrt(square / D + 1e-6)
    nrm[...] = (res[...] * scale * gain_ref[...]).astype(BF16)

    expert = lax.div(ctx, 2)
    route = jnp.sum(gw_ref[...] * (ids_ref[...] == expert).astype(F32), axis=0, keepdims=True)
    row = lax.broadcasted_iota(jnp.int32, (8, HYPS), 0)
    col = lax.broadcasted_iota(jnp.int32, (8, HYPS), 1)
    route = jnp.sum(jnp.where(col == row + 8 * k, route, 0.0), axis=1, keepdims=True)
    for copy in own_w[2:]:
        copy.wait()
    for copy in got_w[2:]:
        copy.wait_recv()
    gate = lax.dot_general(nrm[...], wg[...], NT, preferred_element_type=F32)
    up = lax.dot_general(nrm[...], wu[...], NT, preferred_element_type=F32)
    act = (gate / (1.0 + jnp.exp(-gate)) * up * route).astype(BF16)
    start = x * 1792 + z * 224 + y * 56
    lane = lax.broadcasted_iota(jnp.int32, (8, 128), 1)
    for b in range(4):
        tiles = []
        for t in range(14):
            cols = slice(1792 * b + 128 * t, 1792 * b + 128 * t + 128)
            if t % 7 == 0:
                wide = slice(cols.start, cols.start + 896)
                term = jnp.dot(act, wd[:, wide], preferred_element_type=F32)
            col = lane + cols.start
            mine = (col >= start) & (col < start + 56)
            piece = term[:, 128 * (t % 7) : 128 * (t % 7) + 128]
            tiles.append(piece + jnp.where(mine, res[:, cols], 0.0))
        for c in range(4):
            halves = [
                jnp.where(
                    lane < 64,
                    window(tiles, 448 * u + 56 * c, 0),
                    window(tiles, 448 * u + 224 + 56 * c, 64),
                )
                for u in range(4)
            ]
            whole = jnp.concatenate(halves, axis=1)
            e1f[4 * b + c] = whole
            esb[4 * b + c] = jnp.concatenate([whole[:, :256], whole[:, 256:]], axis=0).astype(BF16)
    got = []
    for j, (dx, dy) in enumerate(XY):
        to = lax.rem(x + dx, 4) * 4 + lax.rem(y + dy, 4)
        got.append(remote(esb.at[to], er1.at[j], dev(dx=dx, dy=dy)))
    for copy in got:
        copy.wait_recv()
    part = er1[0].astype(F32)
    for j in range(1, 15):
        part = part + er1[j].astype(F32)
    part = jnp.concatenate([part[:8], part[8:]], axis=1) + e1f[me]
    for b in range(8):
        tile = part[:, 128 * (b // 2) : 128 * (b // 2) + 128]
        for c in range(2):
            off = 64 * (b % 2) + 28 * c
            e2b[2 * b + c] = pltpu.roll(tile, 128 - off, 1) if off else tile
    got = []
    for j, (dz, dk) in enumerate(ZK):
        to = lax.rem(z + dz, 8) * 2 + lax.rem(k + dk, 2)
        got.append(remote(e2b.at[to], er2.at[j], dev(dz=dz, dk=dk)))
    for copy in got:
        copy.wait_recv()
    same, other = e2b[2 * z + k], jnp.zeros((8, 128), F32)
    for j, (dz, dk) in enumerate(ZK):
        if dk:
            other = other + er2[j]
        else:
            same = same + er2[j]
    both = jnp.concatenate(
        [jnp.where(k == 0, same, other), jnp.where(k == 0, other, same)], axis=0
    )
    upd_ref[...] = both[:, :28].astype(BF16)

    got_att.wait_recv()
    for b in range(8):
        a, o = c3[b].astype(F32), c3o[b].astype(F32)
        first, second = jnp.where(k == 0, a, o), jnp.where(k == 0, o, a)
        for half, width in ((0, 512), (1, 384)):
            cols = slice(896 * b + 512 * half, 896 * b + 512 * half + width)
            rows = slice(8 * half, 8 * half + 8)
            pair = jnp.concatenate([first[rows, :width], second[rows, :width]], axis=0)
            att_ref[:, cols] = pair.astype(BF16)
    for copy in sends:
        copy.wait_send()


def local(
    query_latent, query_rope, cache_latent, cache_rope, suffix_latent, suffix_rope, lengths,
    parents, w_uv, w_o, hidden, norm_gain, w_gate, w_up, w_down, expert_ids, gate_weights,
):
    hbm = pl.BlockSpec(memory_space=pltpu.HBM)
    vmem = pl.BlockSpec(memory_space=pltpu.VMEM)
    scratch = [
        ((HYPS, D), BF16),
        ((1, D), F32),
        ((8, HYPS), jnp.int32),
        ((8, HYPS), F32),
        ((HYPS, 16 * DR), BF16),
        ((256, 128), F32),
        ((2, 4, 16, DL + 128), BF16),
        ((4, 128, DL + 128), BF16),
        ((4, 128, DL), BF16),
        ((2, 1024, DL), BF16),
        ((2, 2 * DR, 1024), BF16),
        ((4, 256, DL), BF16),
        ((4, 256, DL), BF16),
        ((4, 2 * DR, 256), BF16),
        ((4, 2 * DR, 256), BF16),
        ((2, 64, DL), BF16),
        ((128, D), BF16),
        ((256, D), BF16),
        ((256, D), BF16),
        ((256, D), BF16),
        ((4, 4, HEADS, 128), F32),
        ((HEADS, 128), F32),
        ((2, 16, 32, DL), BF16),
        ((2, 16, 8, 128), F32),
        ((2, 15, 32, DL), BF16),
        ((2, 15, 8, 128), F32),
        ((5, 64, 128), F32),
        ((8, 8, 640), F32),
        ((7, 8, 640), F32),
        ((8, 16, 512), BF16),
        ((7, 16, 512), BF16),
        ((16, 16, 512), BF16),
        ((8, 16, 512), BF16),
        ((8, 16, 512), BF16),
        ((8, D), F32),
        ((8, D), BF16),
        ((16, 8, 512), F32),
        ((16, 16, 256), BF16),
        ((15, 16, 256), BF16),
        ((16, 8, 128), F32),
        ((15, 8, 128), F32),
    ]
    return pl.pallas_call(
        kernel,
        name="decode_step",
        out_shape=(
            jax.ShapeDtypeStruct((HYPS, D), BF16),
            jax.ShapeDtypeStruct((HYPS, 28), BF16),
        ),
        in_specs=[hbm] * 17,
        out_specs=(vmem, vmem),
        scratch_shapes=[pltpu.VMEM(shape, dtype) for shape, dtype in scratch]
        + [
            pltpu.SMEM((4,), jnp.int32),
            pltpu.SMEM((16,), jnp.int32),
            pltpu.SemaphoreType.DMA((N_SEMS,)),
            pltpu.SemaphoreType.DMA((N_SEMS,)),
            pltpu.SemaphoreType.DMA((N_LOCAL,)),
        ],
        compiler_params=pltpu.CompilerParams(
            collective_id=0, has_side_effects=True, vmem_limit_bytes=48 << 20
        ),
    )(
        *(
            pltpu.with_memory_space_constraint(value, pltpu.HBM)
            for value in (
                query_latent, query_rope, cache_latent, cache_rope, suffix_latent, suffix_rope,
                w_uv.T, w_o, w_gate, w_up, w_down, lengths, parents, hidden,
                norm_gain.reshape(1, D), expert_ids.T, gate_weights.T,
            )
        )
    )


def solution(mesh):
    both = ("ctx", "hx")
    in_specs = (
        P(None, "hx", None),
        P(None, "hx"),
        P(None, both, None),
        P(None, None, both),
        P(None, both, None),
        P(None, None, both),
        P(),
        P(),
        P(None, both),
        P(both, None),
        P(),
        P(),
        P(both, None),
        P(both, None),
        P(both, None),
        P(),
        P(),
    )
    out_specs = (P(), P(None, both))
    return jax.shard_map(local, mesh=mesh, in_specs=in_specs, out_specs=out_specs, check_vma=False)
```

time: 97.7 us -> 77.3 us (0.79)
  local copies, waits for them, and re-layouts: 13.7 us -> 1.28 us
  Pallas kernels: 81.8 us -> 75.3 us
  other arithmetic: 0.98 us -> 0 us
    unnamed x23 -> x2, local copies, waits for them, and re-layouts: 12.8 us -> 1.28 us
    pallas_call x1, Pallas kernels: 81.8 us -> 75.3 us  [local(): pl.pallas_call(kernel, name='decode_step', out_shape=(jax.ShapeDtypeStruc...]
    concatenate x1 -> x0, other arithmetic: 0.98 us -> none  [local(): jnp.concatenate([query_latent, query_rope.reshape(HYPS, 16, DR)], axis=2)]
where the time goes in v2:
time: 77.3 us; the launch traced here: 77.2 us
  Pallas kernels  75.3 us (97%)
  local copies, waits for them, and re-layouts  1.28 us (2%)
    pallas_call x1, Pallas kernels, local(): pl.pallas_call(kernel, name='decode_step', out_shape=(jax.ShapeDtypeStruc...  75.3 us

profile of v2, /device:TPU:1, one launch (start us, length us, event | category | flops | bytes accessed | tf_op | source)
XLA Modules:
  0.0 77.2 jit_solution(17382064385168314682)
XLA Ops:
  0.6 75.3 %decode_step.1 = (bf16[16,7168]{1,0:T(8,128)(2,1)S(1)}, bf16[16,28]{1,0:T(8,128)(2,1)S(1)}) custom-call(bf16[16,16,512]{2,1,0:T(8,128)(2,1)} %ql_hbm.1, bf16[16,1024]{1,0:T(8,128)(2,1)} %qr_hbm.1, bf16[4,512,512]{2,1,0:T(8,128)(2,1)} %ck_hbm.1, bf16[4,64,512]{2,1,0:T(8,128)(2,1)} %cr_hbm.1, bf16[16,128,512]{2,1,0:T(8,128)(2,1)} %sl_hbm.1, ...), custom_call_target="tpu_custom_call" | custom-call | tf_op jit(solution)/shard_map/decode_step/pallas_call | solution.py:467
  75.9 0.7 copy.21
  76.6 0.6 copy.22

commit v3 on v2

--- a/solution.py
+++ b/solution.py
@@ -68,7 +68,7 @@
     hid_ref, gain_ref, ids_ref, gw_ref, rope, ropes, qc, qv0, qv1, kv, kr, s0, s1, sr0, sr1,
     wuv, wo, wg, wu, wd, tmp, st, ob, osb, br, bsr, zt, zsb, zr,
     csb, cr1, c2, c3, c3o, res, nrm, e1f, esb, er1, e2b, er2,
-    len_ref, par_ref, ss, rs, ls,
+    len_ref, par_ref, ss, rs, ls, here,
 ):
     ctx, hx = lax.axis_index("ctx"), lax.axis_index("hx")
     x, z = lax.div(ctx, 8), lax.rem(ctx, 8)
@@ -132,9 +132,8 @@
     ZK = [(dz, dk) for dz in (4, 3, 5, 2, 6, 1, 7, 0) for dk in range(2) if dz or dk]
 
     barrier = pltpu.get_barrier_semaphore()
-    peers = [dev(dz=dz, dk=dk) for dz, dk in ZK]
-    peers += [dev(dx=dx, dy=dy) for dx, dy in XY]
-    peers += [dev(dy=dy, dk=1) for dy in range(1, 4)]
+    near = [dev(dx=1), dev(dx=3), dev(dz=1), dev(dz=7)]
+    peers = [dev(dy=dy, dk=dk) for dy, dk in HX] + near
     for peer in peers:
         pl.semaphore_signal(barrier, inc=1, device_id=peer, device_id_type=MESH)
     own_q = [local(qr_hbm, rope)]
@@ -165,6 +164,13 @@
     own[0].append(local(qc.at[k], qv0.at[:, head_rows]))
     pl.semaphore_wait(barrier, len(peers))
 
+    def tell(i):
+        for peer in near:
+            pl.semaphore_signal(here.at[i], inc=1, device_id=peer, device_id_type=MESH)
+
+    def hear(i):
+        pl.semaphore_wait(here.at[i], len(near))
+
     beam = lax.rem(x + 2 * z, 4)
     got_q = {}
     for dy, dk in HX:
@@ -174,6 +180,7 @@
         else:
             src, dst = qc.at[core], qv0.at[:, head_rows]
         got_q[dy, dk] = remote(src, dst, dev(dy=dy, dk=dk))
+    tell(0)
     got_in = [[got_q[0, 1]], []]
     for src, dst in kv_pairs(0, kk):
         got_in[0].append(remote(src, dst, dev(dk=1)))
@@ -185,6 +192,8 @@
         for where in (dev(dx=1), dev(dx=3), dev(dz=1)):
             got_in[0].append(remote(block, block, where))
 
+    hear(0)
+    tell(1)
     for dy, dk in HX:
         core = lax.rem(k + dk, 2)
         src = ql_hbm.at[pl.ds(8 * core + 4, 4)]
@@ -261,10 +270,15 @@
                 zt[l, at] = acc[:, 128 * l : 128 * l + 128]
             zt[4, at] = stat_lanes([top[:, i : i + 1], total[:, 4 + i : 5 + i]], 8)
 
+    hear(1)
+    tell(2)
     attend(0)
+    hear(2)
+    tell(3)
     got_b0 = join_send(0)
     got_w = [remote(src, dst, dev(dk=1)) for src, dst in w_pairs]
     attend(1)
+    hear(3)
     got_b1 = join_send(1)
     join(0, got_b0)
     join(1, got_b1)
@@ -288,14 +302,15 @@
         copy.wait_recv()
     v0 = lax.dot_general(attention, wuv[0], NT, preferred_element_type=F32).astype(BF16)
     v1 = lax.dot_general(attention, wuv[1], NT, preferred_element_type=F32).astype(BF16)
-    for b in range(8):
-        cols = slice(896 * b, 896 * b + 896)
+    got = []
+    for dz in (4, 3, 5, 2, 6, 1, 7, 0):
+        b = lax.rem(z + dz, 8)
+        cols = pl.ds(pl.multiple_of(b * 896, 128), 896)
         term = jnp.dot(v0, wo[:64, cols], preferred_element_type=F32)
         term = term + jnp.dot(v1, wo[64:, cols], preferred_element_type=F32)
         csb[b] = pack896(term).astype(BF16)
-    got = []
-    for dz in (4, 3, 5, 2, 6, 1, 7):
-        got.append(remote(csb.at[lax.rem(z + dz, 8)], cr1.at[dz - 1], dev(dz=dz)))
+        if dz:
+            got.append(remote(csb.at[b], cr1.at[dz - 1], dev(dz=dz)))
     for copy in got:
         copy.wait_recv()
     part = csb[z].astype(F32)
@@ -347,17 +362,22 @@
     act = (gate / (1.0 + jnp.exp(-gate)) * up * route).astype(BF16)
     start = x * 1792 + z * 224 + y * 56
     lane = lax.broadcasted_iota(jnp.int32, (8, 128), 1)
-    for b in range(4):
+    got = []
+    for dx in (2, 1, 3, 0):
+        b = lax.rem(x + dx, 4)
         tiles = []
         for t in range(14):
-            cols = slice(1792 * b + 128 * t, 1792 * b + 128 * t + 128)
+            at = b * 1792 + 128 * t
             if t % 7 == 0:
-                wide = slice(cols.start, cols.start + 896)
+                wide = pl.ds(pl.multiple_of(at, 128), 896)
                 term = jnp.dot(act, wd[:, wide], preferred_element_type=F32)
-            col = lane + cols.start
-            mine = (col >= start) & (col < start + 56)
             piece = term[:, 128 * (t % 7) : 128 * (t % 7) + 128]
-            tiles.append(piece + jnp.where(mine, res[:, cols], 0.0))
+            if dx == 0:
+                col = lane + at
+                mine = (col >= start) & (col < start + 56)
+                rest = res[:, pl.ds(pl.multiple_of(at, 128), 128)]
+                piece = piece + jnp.where(mine, rest, 0.0)
+            tiles.append(piece)
         for c in range(4):
             halves = [
                 jnp.where(
@@ -368,18 +388,28 @@
                 for u in range(4)
             ]
             whole = jnp.concatenate(halves, axis=1)
-            e1f[4 * b + c] = whole
+            if dx == 0:
+                e1f[c] = whole
             esb[4 * b + c] = jnp.concatenate([whole[:, :256], whole[:, 256:]], axis=0).astype(BF16)
-    got = []
-    for j, (dx, dy) in enumerate(XY):
-        to = lax.rem(x + dx, 4) * 4 + lax.rem(y + dy, 4)
-        got.append(remote(esb.at[to], er1.at[j], dev(dx=dx, dy=dy)))
+        for dy in (2, 1, 3, 0):
+            if dx or dy:
+                to = 4 * b + lax.rem(y + dy, 4)
+                got.append(remote(esb.at[to], er1.at[4 * dx + dy - 1], dev(dx=dx, dy=dy)))
+    got_att.wait_recv()
+    for b in range(8):
+        a, o = c3[b].astype(F32), c3o[b].astype(F32)
+        first, second = jnp.where(k == 0, a, o), jnp.where(k == 0, o, a)
+        for half, width in ((0, 512), (1, 384)):
+            cols = slice(896 * b + 512 * half, 896 * b + 512 * half + width)
+            rows = slice(8 * half, 8 * half + 8)
+            pair = jnp.concatenate([first[rows, :width], second[rows, :width]], axis=0)
+            att_ref[:, cols] = pair.astype(BF16)
     for copy in got:
         copy.wait_recv()
     part = er1[0].astype(F32)
     for j in range(1, 15):
         part = part + er1[j].astype(F32)
-    part = jnp.concatenate([part[:8], part[8:]], axis=1) + e1f[me]
+    part = jnp.concatenate([part[:8], part[8:]], axis=1) + e1f[y]
     for b in range(8):
         tile = part[:, 128 * (b // 2) : 128 * (b // 2) + 128]
         for c in range(2):
@@ -402,15 +432,6 @@
     )
     upd_ref[...] = both[:, :28].astype(BF16)
 
-    got_att.wait_recv()
-    for b in range(8):
-        a, o = c3[b].astype(F32), c3o[b].astype(F32)
-        first, second = jnp.where(k == 0, a, o), jnp.where(k == 0, o, a)
-        for half, width in ((0, 512), (1, 384)):
-            cols = slice(896 * b + 512 * half, 896 * b + 512 * half + width)
-            rows = slice(8 * half, 8 * half + 8)
-            pair = jnp.concatenate([first[rows, :width], second[rows, :width]], axis=0)
-            att_ref[:, cols] = pair.astype(BF16)
     for copy in sends:
         copy.wait_send()
 
@@ -458,7 +479,7 @@
         ((8, 16, 512), BF16),
         ((8, D), F32),
         ((8, D), BF16),
-        ((16, 8, 512), F32),
+        ((4, 8, 512), F32),
         ((16, 16, 256), BF16),
         ((15, 16, 256), BF16),
         ((16, 8, 128), F32),
@@ -480,6 +501,7 @@
             pltpu.SemaphoreType.DMA((N_SEMS,)),
             pltpu.SemaphoreType.DMA((N_SEMS,)),
             pltpu.SemaphoreType.DMA((N_LOCAL,)),
+            pltpu.SemaphoreType.REGULAR((4,)),
         ],
         compiler_params=pltpu.CompilerParams(
             collective_id=0, has_side_effects=True, vmem_limit_bytes=48 << 20

time: 77.3 us -> 75.2 us (0.973)
  Pallas kernels: 75.3 us -> 73.2 us
    pallas_call x1, Pallas kernels: 75.3 us -> 73.2 us  [local(): pl.pallas_call(kernel, name='decode_step', out_shape=(jax.ShapeDtypeStruc...]
where the time goes in v3:
time: 75.2 us; the launch traced here: 75.1 us
  Pallas kernels  73.2 us (97%)
  local copies, waits for them, and re-layouts  1.28 us (2%)
    pallas_call x1, Pallas kernels, local(): pl.pallas_call(kernel, name='decode_step', out_shape=(jax.ShapeDtypeStruc...  73.2 us

profile of v3, /device:TPU:1, one launch (start us, length us, event | category | flops | bytes accessed | tf_op | source)
XLA Modules:
  0.0 75.1 jit_solution(8250402602242952032)
XLA Ops:
  0.6 73.2 %decode_step.1 = (bf16[16,7168]{1,0:T(8,128)(2,1)S(1)}, bf16[16,28]{1,0:T(8,128)(2,1)S(1)}) custom-call(bf16[16,16,512]{2,1,0:T(8,128)(2,1)} %ql_hbm.1, bf16[16,1024]{1,0:T(8,128)(2,1)} %qr_hbm.1, bf16[4,512,512]{2,1,0:T(8,128)(2,1)} %ck_hbm.1, bf16[4,64,512]{2,1,0:T(8,128)(2,1)} %cr_hbm.1, bf16[16,128,512]{2,1,0:T(8,128)(2,1)} %sl_hbm.1, ...), custom_call_target="tpu_custom_call" | custom-call | tf_op jit(solution)/shard_map/decode_step/pallas_call | solution.py:488
  73.8 0.7 copy.21
  74.5 0.6 copy.22

commit v4 on v3

--- a/solution.py
+++ b/solution.py
@@ -23,7 +23,7 @@
 NEG = -1e30
 NT = (((1,), (1,)), ((), ()))
 
-N_SEMS = 168
+N_SEMS = 184
 N_LOCAL = 24
 
 
@@ -126,7 +126,7 @@
         (wd_hbm, wd.at[unit_rows]),
     )
 
-    HX = [(dy, dk) for dy in (1, 3, 2, 0) for dk in range(2) if dy or dk]
+    HX = [(dy, dk) for dy in (2, 1, 3, 0) for dk in range(2) if dy or dk]
     XY = [(dx, dy) for dx in range(4) for dy in range(4) if dx or dy]
     XY.sort(key=lambda d: -min(d[0], 4 - d[0]) - min(d[1], 4 - d[1]))
     ZK = [(dz, dk) for dz in (4, 3, 5, 2, 6, 1, 7, 0) for dk in range(2) if dz or dk]
@@ -200,25 +200,20 @@
         got_in[1].append(remote(src, qv1.at[:, head_rows], dev(dy=dy, dk=dk)))
     for src, dst in kv_pairs(1, kk):
         got_in[1].append(remote(src, dst, dev(dk=1)))
-    def attend(r):
-        for copy in own[r]:
-            copy.wait()
-        for copy in got_in[r]:
-            copy.wait_recv()
-        q = qv0[..., :DL] if r == 0 else qv1[...]
-        qr = qv0[..., DL:]
-        ql = q.reshape(4 * HEADS, DL)
-        s = lax.dot_general(ql, kv[r], NT, preferred_element_type=F32)
-        s = s + jnp.dot(
-            qr.reshape(4 * HEADS, 128), kr[r], preferred_element_type=F32
-        )
+    def attend(r, beams):
+        few = len(beams)
+        first = beams[0]
+        q = (qv1 if r else qv0)[first : first + few, :, :DL]
+        qr = qv0[first : first + few, :, DL:]
+        s = lax.dot_general(q.reshape(few * HEADS, DL), kv[r], NT, preferred_element_type=F32)
+        s = s + jnp.dot(qr.reshape(few * HEADS, 128), kr[r], preferred_element_type=F32)
         pos = chip * 1024 + lax.broadcasted_iota(jnp.int32, (1, 1024), 1)
         s = jnp.where(pos < len_ref[2 * k + r], s * SCALE, NEG)
         high = jnp.max(s, axis=1, keepdims=True)
-        rows = [slice(i * HEADS, (i + 1) * HEADS) for i in range(4)]
+        rows = [slice(i * HEADS, (i + 1) * HEADS) for i in range(few)]
         own_s, tops, parent = [], [], []
-        for i in range(4):
-            p = lax.rem(par_ref[8 * k + 4 * r + i], 4)
+        for i in range(few):
+            p = lax.rem(par_ref[8 * k + 4 * r + first + i], 4)
             si = lax.dot_general(q[i], sv[r][p], NT, preferred_element_type=F32)
             si = si + jnp.dot(qr[i], srv[r][p], preferred_element_type=F32)
             own_s.append(si * SCALE)
@@ -228,33 +223,52 @@
         total = jnp.sum(w.astype(F32), axis=1, keepdims=True)
         acc = jnp.dot(w, kv[r], preferred_element_type=F32)
         totals = []
-        for i in range(4):
+        for i in range(few):
             wi = jnp.exp2(own_s[i] - tops[i]).astype(BF16)
             totals.append(total[rows[i]] + jnp.sum(wi.astype(F32), axis=1, keepdims=True))
             ai = acc[rows[i]] + jnp.dot(wi, sv[r][parent[i]], preferred_element_type=F32)
             for l in range(4):
                 tmp[i, l] = ai[:, 128 * l : 128 * l + 128]
-        st[...] = stat_lanes(tops + totals, HEADS)
+        none = [0.0] * first
+        rest = [0.0] * (4 - few - first)
+        lane = lax.broadcasted_iota(jnp.int32, (HEADS, 128), 1)
+        row = lax.broadcasted_iota(jnp.int32, (HEADS, 128), 0)
+        lane = lane - 8 * jnp.bitwise_and(jnp.right_shift(row, 2), 7)
+        stat = jnp.zeros((HEADS, 128), F32)
+        for j, figure in enumerate(none + tops + rest + none + totals + rest):
+            if not isinstance(figure, float):
+                stat = jnp.where(lane == j, figure, stat)
+        st[...] = st[...] + stat if first else stat
         for to in range(16):
             pick = pl.ds(32 * (to // 4) + to % 4, 8, stride=4)
             for l in range(4):
-                block = jnp.concatenate([tmp[i, l, pick, :] for i in range(4)], axis=0)
-                ob[r, to, :, 128 * l : 128 * l + 128] = block.astype(BF16)
-            osb[r, to] = st[pick, :]
+                block = jnp.concatenate([tmp[i, l, pick, :] for i in range(few)], axis=0)
+                lanes = slice(128 * l, 128 * l + 128)
+                ob[r, to, 8 * first : 8 * (first + few), lanes] = block.astype(BF16)
+            if first + few == 4:
+                osb[r, to] = jnp.sum(st[pick, :], axis=0, keepdims=True)
 
     me = x * 4 + y
 
-    def join_send(r):
+    def join_send(r, beams):
         got = []
+        rows = pl.ds(8 * beams[0], 8 * len(beams))
         for j, (dx, dy) in enumerate(XY):
             to = lax.rem(x + dx, 4) * 4 + lax.rem(y + dy, 4)
-            got.append(remote(osb.at[r, to], bsr.at[r, j], dev(dx=dx, dy=dy)))
-            got.append(remote(ob.at[r, to], br.at[r, j], dev(dx=dx, dy=dy)))
+            if beams[-1] == 3:
+                got.append(remote(osb.at[r, to], bsr.at[r, j], dev(dx=dx, dy=dy)))
+            got.append(remote(ob.at[r, to, rows], br.at[r, j, rows], dev(dx=dx, dy=dy)))
         return got
 
     def join(r, got):
         for copy in got:
             copy.wait_recv()
+        lane = lax.broadcasted_iota(jnp.int32, (8, 128), 1)
+        lane = lane - 8 * lax.broadcasted_iota(jnp.int32, (8, 128), 0)
+
+        def column(figures, j):
+            return jnp.sum(jnp.where(lane == j, figures, 0.0), axis=1, keepdims=True)
+
         stats = [osb[r, me]] + [bsr[r, j] for j in range(15)]
         top = functools.reduce(jnp.maximum, stats)
         factors = [jnp.exp2(stat - top) for stat in stats]
@@ -264,22 +278,32 @@
             for j in range(16):
                 block = ob[r, me] if j == 0 else br[r, j - 1]
                 rows = block.astype(F32)[8 * i : 8 * i + 8]
-                acc = acc + rows * factors[j][:, i : i + 1]
+                acc = acc + rows * column(factors[j], i)
             at = pl.ds((4 * r + i) * 8, 8)
             for l in range(4):
                 zt[l, at] = acc[:, 128 * l : 128 * l + 128]
-            zt[4, at] = stat_lanes([top[:, i : i + 1], total[:, 4 + i : 5 + i]], 8)
+            zt[4, at] = stat_lanes([column(top, i), column(total, 4 + i)], 8)
 
     hear(1)
     tell(2)
-    attend(0)
+    for copy in own[0]:
+        copy.wait()
+    for copy in got_in[0]:
+        copy.wait_recv()
+    attend(0, [0, 1])
+    got_b0 = join_send(0, [0, 1])
+    attend(0, [2, 3])
     hear(2)
     tell(3)
-    got_b0 = join_send(0)
+    got_b0 += join_send(0, [2, 3])
     got_w = [remote(src, dst, dev(dk=1)) for src, dst in w_pairs]
-    attend(1)
+    for copy in own[1]:
+        copy.wait()
+    for copy in got_in[1]:
+        copy.wait_recv()
+    attend(1, [0, 1, 2, 3])
     hear(3)
-    got_b1 = join_send(1)
+    got_b1 = join_send(1, [0, 1, 2, 3])
     join(0, got_b0)
     join(1, got_b1)
     for b in range(8):
@@ -466,9 +490,9 @@
         ((4, 4, HEADS, 128), F32),
         ((HEADS, 128), F32),
         ((2, 16, 32, DL), BF16),
-        ((2, 16, 8, 128), F32),
+        ((2, 16, 1, 128), F32),
         ((2, 15, 32, DL), BF16),
-        ((2, 15, 8, 128), F32),
+        ((2, 15, 1, 128), F32),
         ((5, 64, 128), F32),
         ((8, 8, 640), F32),
         ((7, 8, 640), F32),

time: 75.2 us -> 73.6 us (0.979)
  Pallas kernels: 73.2 us -> 71.6 us
    pallas_call x1, Pallas kernels: 73.2 us -> 71.6 us  [local(): pl.pallas_call(kernel, name='decode_step', out_shape=(jax.ShapeDtypeStruc...]
where the time goes in v4:
time: 73.6 us; the launch traced here: 73.5 us
  Pallas kernels  71.6 us (97%)
  local copies, waits for them, and re-layouts  1.28 us (2%)
    pallas_call x1, Pallas kernels, local(): pl.pallas_call(kernel, name='decode_step', out_shape=(jax.ShapeDtypeStruc...  71.6 us

profile of v4, /device:TPU:1, one launch (start us, length us, event | category | flops | bytes accessed | tf_op | source)
XLA Modules:
  0.0 73.5 jit_solution(11261146724254594113)
XLA Ops:
  0.6 71.6 %decode_step.1 = (bf16[16,7168]{1,0:T(8,128)(2,1)S(1)}, bf16[16,28]{1,0:T(8,128)(2,1)S(1)}) custom-call(bf16[16,16,512]{2,1,0:T(8,128)(2,1)} %ql_hbm.1, bf16[16,1024]{1,0:T(8,128)(2,1)} %qr_hbm.1, bf16[4,512,512]{2,1,0:T(8,128)(2,1)} %ck_hbm.1, bf16[4,64,512]{2,1,0:T(8,128)(2,1)} %cr_hbm.1, bf16[16,128,512]{2,1,0:T(8,128)(2,1)} %sl_hbm.1, ...), custom_call_target="tpu_custom_call" | custom-call | tf_op jit(solution)/shard_map/decode_step/pallas_call | solution.py:512
  72.2 0.7 copy.21
  72.9 0.6 copy.22

commit v5 on v4

--- a/solution.py
+++ b/solution.py
@@ -23,7 +23,7 @@
 NEG = -1e30
 NT = (((1,), (1,)), ((), ()))
 
-N_SEMS = 184
+N_SEMS = 192
 N_LOCAL = 24
 
 
@@ -66,7 +66,7 @@
     len_hbm, par_hbm, hid_hbm, gain_hbm, ids_hbm, gw_hbm,
     att_ref, upd_ref,
     hid_ref, gain_ref, ids_ref, gw_ref, rope, ropes, qc, qv0, qv1, kv, kr, s0, s1, sr0, sr1,
-    wuv, wo, wg, wu, wd, tmp, st, ob, osb, br, bsr, zt, zsb, zr,
+    wuv, wo, wg, wu, wd, tmp, st, ob, osb, br, bsr, zt, zsb, zss, zr, zrs,
     csb, cr1, c2, c3, c3o, res, nrm, e1f, esb, er1, e2b, er2,
     len_ref, par_ref, ss, rs, ls, here,
 ):
@@ -93,6 +93,11 @@
         copy.start()
         sends.append(copy)
         return copy
+
+    def flush():
+        for copy in sends:
+            copy.wait_send()
+        sends.clear()
 
     def local(src, dst):
         i = count[1]
@@ -307,16 +312,22 @@
     join(0, got_b0)
     join(1, got_b1)
     for b in range(8):
-        for l in range(5):
-            zsb[b, :, 128 * l : 128 * l + 128] = zt[l, pl.ds(b, 8, stride=8), :]
+        pick = pl.ds(b, 8, stride=8)
+        for l in range(2):
+            block = jnp.concatenate([zt[l, pick, :], zt[l + 2, pick, :]], axis=0)
+            zsb[b, :, 128 * l : 128 * l + 128] = block.astype(BF16)
+        zss[b] = zt[4, pick, :]
     got = []
     for dz in (4, 3, 5, 2, 6, 1, 7):
-        got.append(remote(zsb.at[lax.rem(z + dz, 8)], zr.at[dz - 1], dev(dz=dz)))
+        to = lax.rem(z + dz, 8)
+        got.append(remote(zss.at[to], zrs.at[dz - 1], dev(dz=dz)))
+        got.append(remote(zsb.at[to], zr.at[dz - 1], dev(dz=dz)))
     for copy in got:
         copy.wait_recv()
     parts = []
-    for a in [zsb[z]] + [zr[j] for j in range(7)]:
-        parts.append((a[:, DL : DL + 1], a[:, DL + 1 : DL + 2], a[:, :DL]))
+    for a, t in [(zsb[z], zss[z])] + [(zr[j], zrs[j]) for j in range(7)]:
+        a = a.astype(F32)
+        parts.append((t[:, :1], t[:, 1:2], jnp.concatenate([a[:8], a[8:]], axis=1)))
     top, total, acc = fold(parts)
     attention = (acc / total).astype(BF16)
 
@@ -335,6 +346,7 @@
         csb[b] = pack896(term).astype(BF16)
         if dz:
             got.append(remote(csb.at[b], cr1.at[dz - 1], dev(dz=dz)))
+    flush()
     for copy in got:
         copy.wait_recv()
     part = csb[z].astype(F32)
@@ -344,6 +356,7 @@
     got = []
     for dx, dy in XY:
         got.append(remote(c2.at[me], c2.at[me], dev(dx=dx, dy=dy)))
+    flush()
     for copy in got:
         copy.wait_recv()
     part = c2[0].astype(F32)
@@ -428,6 +441,7 @@
             rows = slice(8 * half, 8 * half + 8)
             pair = jnp.concatenate([first[rows, :width], second[rows, :width]], axis=0)
             att_ref[:, cols] = pair.astype(BF16)
+    flush()
     for copy in got:
         copy.wait_recv()
     part = er1[0].astype(F32)
@@ -443,6 +457,7 @@
     for j, (dz, dk) in enumerate(ZK):
         to = lax.rem(z + dz, 8) * 2 + lax.rem(k + dk, 2)
         got.append(remote(e2b.at[to], er2.at[j], dev(dz=dz, dk=dk)))
+    flush()
     for copy in got:
         copy.wait_recv()
     same, other = e2b[2 * z + k], jnp.zeros((8, 128), F32)
@@ -456,8 +471,7 @@
     )
     upd_ref[...] = both[:, :28].astype(BF16)
 
-    for copy in sends:
-        copy.wait_send()
+    flush()
 
 
 def local(
@@ -494,8 +508,10 @@
         ((2, 15, 32, DL), BF16),
         ((2, 15, 1, 128), F32),
         ((5, 64, 128), F32),
-        ((8, 8, 640), F32),
-        ((7, 8, 640), F32),
+        ((8, 16, 256), BF16),
+        ((8, 8, 128), F32),
+        ((7, 16, 256), BF16),
+        ((7, 8, 128), F32),
         ((8, 16, 512), BF16),
         ((7, 16, 512), BF16),
         ((16, 16, 512), BF16),

time: 73.6 us -> 72.2 us (0.981)
  Pallas kernels: 71.6 us -> 70.2 us
    pallas_call x1, Pallas kernels: 71.6 us -> 70.2 us  [local(): pl.pallas_call(kernel, name='decode_step', out_shape=(jax.ShapeDtypeStruc...]
where the time goes in v5:
time: 72.2 us; the launch traced here: 72.1 us
  Pallas kernels  70.2 us (97%)
  local copies, waits for them, and re-layouts  1.28 us (2%)
    pallas_call x1, Pallas kernels, local(): pl.pallas_call(kernel, name='decode_step', out_shape=(jax.ShapeDtypeStruc...  70.2 us

profile of v5, /device:TPU:1, one launch (start us, length us, event | category | flops | bytes accessed | tf_op | source)
XLA Modules:
  0.0 72.1 jit_solution(13474583368935806626)
XLA Ops:
  0.6 70.2 %decode_step.1 = (bf16[16,7168]{1,0:T(8,128)(2,1)S(1)}, bf16[16,28]{1,0:T(8,128)(2,1)S(1)}) custom-call(bf16[16,16,512]{2,1,0:T(8,128)(2,1)} %ql_hbm.1, bf16[16,1024]{1,0:T(8,128)(2,1)} %qr_hbm.1, bf16[4,512,512]{2,1,0:T(8,128)(2,1)} %ck_hbm.1, bf16[4,64,512]{2,1,0:T(8,128)(2,1)} %cr_hbm.1, bf16[16,128,512]{2,1,0:T(8,128)(2,1)} %sl_hbm.1, ...), custom_call_target="tpu_custom_call" | custom-call | tf_op jit(solution)/shard_map/decode_step/pallas_call | solution.py:528
  70.9 0.7 copy.21
  71.5 0.6 copy.22
